TPU v7x, 512 devices: a whole 4x8x8 slice. The times are simulated.
512 devices in a mesh: row: 16 (over x_hi, y), col: 32 (over z, x_lo, core).
Axes of the slice: x: 4 (x_hi: 2, x_lo: 2; x = x_hi * 2 + x_lo), y: 8, z: 8, core: 2. Of those that a mesh axis runs over, the one named last changes fastest.
Arguments:
- vectors: bfloat16 [512, 32768], P('row', 'col'), may hold values from -6 to 6
- factor_tiles: bfloat16 [128, 96, 256, 256], P('row', 'col'), may hold values from -0.0546875 to 0.0546875
- tile_columns: int32 [128, 96], P('row', 'col'), may hold values from 0 to 127, as said below
- live_counts: int32 [128, 32], P('row', 'col'), may hold values from 0 to 3, as said below
Outputs:
- applied: float32 [512, 32768], P('row', 'col')
Inputs may be any that keep to these rules, and one draw needn't show every extreme that they name: `tile_columns`: slot s holds a tile column in [(s // 3) * 4, (s // 3 + 1) * 4); the slots of one row tile name distinct columns; a live slot's column is at most its row tile; the row tile's own column is always live, in the first slot of its group. `live_counts`: counts never exceed the columns allowed in that group, so the upper right region of groups is empty. In group 0 every row tile i >= 2 has exactly 3 live slots.
All inputs are finite; a program needn't handle non-finite values.
Results may differ from a plain program's by a relative error of at most 0.002.
Values may be sent and summed in bfloat16 or wider, within the bound.
No kernel may reach another device: no remote copies, remote signals or barrier semaphores. Data moves between devices by JAX's collectives and lax.ppermute only.
A program may use at most 64 MiB of HBM per device.

v0:
```python
import jax
import jax.numpy as jnp
from jax import lax
from jax.sharding import PartitionSpec as P


def laid_out(tiles, dim):
    tiles = jnp.moveaxis(tiles, 0, dim)
    dims = tiles.shape
    return tiles.reshape(*dims[:dim], dims[dim] * dims[dim + 1], *dims[dim + 2 :])


def from_everyone(shard, axis):
    copies = jnp.broadcast_to(shard, (lax.axis_size(axis), *shard.shape))
    return lax.all_to_all(copies, axis, split_axis=0, concat_axis=0, tiled=True)


def gathered_copies(shard, axis, dim):
    return laid_out(from_everyone(shard, axis), dim)


def split_up(shard, dim, length):
    before, after = (shard.shape[:dim], shard.shape[dim + 1 :])
    return jnp.moveaxis(shard.reshape(*before, length, -1, *after), dim, 0)


def sent_and_summed(shard, axis, dim):
    tiles = split_up(shard, dim, lax.axis_size(axis))
    arrived = lax.all_to_all(tiles, axis, split_axis=0, concat_axis=0, tiled=True)
    return arrived.sum(axis=0)


def per_device(vectors, factor_tiles, tile_columns, live_counts):
    row_tiles = factor_tiles.shape[0]
    slot_count = factor_tiles.shape[1]
    tile_size = factor_tiles.shape[2]
    col_tiles = vectors.shape[1] // tile_size
    offset = lax.axis_index("col") * col_tiles
    local_cols = tile_columns - offset
    slot_index = lax.broadcasted_iota(jnp.int32, (row_tiles, slot_count), 1)
    live_mask = (slot_index < live_counts).astype(jnp.float32)
    column_iota = lax.broadcasted_iota(jnp.int32, (row_tiles, slot_count, col_tiles), 2)
    select_map = (local_cols[:, :, None] == column_iota).astype(jnp.float32) * live_mask[:, :, None]
    select_half = select_map.astype(jnp.bfloat16)
    vector_rows = gathered_copies(vectors, "row", 0)
    count_rows = vector_rows.shape[0]
    blocks = vector_rows.reshape(count_rows, col_tiles, tile_size)
    picked = jnp.einsum(
        "tkj,vjc->tkvc", select_half, blocks, preferred_element_type=jnp.float32
    ).astype(jnp.bfloat16)
    partial_value = jnp.einsum(
        "tkab,tkvb->vta", factor_tiles, picked, preferred_element_type=jnp.float32
    )
    partial_all = partial_value.reshape(count_rows, row_tiles * tile_size)
    rowvals = lax.psum(partial_all, "col").astype(jnp.bfloat16)
    count_rows = rowvals.shape[0]
    weights = rowvals.reshape(count_rows, row_tiles, tile_size)
    contrib = jnp.einsum(
        "tkab,vta->tkvb", factor_tiles, weights, preferred_element_type=jnp.float32
    )
    summed = jnp.einsum("tkj,tkvb->vjb", select_map, contrib, precision=lax.Precision.HIGHEST)
    return sent_and_summed(summed.reshape(count_rows, col_tiles * tile_size), "row", 0)


def solution(mesh):
    in_specs = (P("row", "col"), P("row", "col", None, None), P("row", "col"), P("row", "col"))
    out_specs = P("row", "col")
    return jax.shard_map(
        per_device, mesh=mesh, in_specs=in_specs, out_specs=out_specs, check_vma=False
    )
```

profile of v0, /device:TPU:1, one launch (start us, length us, event | category | flops | bytes accessed | tf_op | source)
XLA Modules:
  0.0 260.5 jit_solution(13637796774997700658)
XLA Ops:
  0.0 0.0 copy-start
  0.0 0.0 copy-start.2
  0.0 0.0 copy-start.1
  0.0 2.2 broadcast_in_dim.2
  2.2 10.3 %all-to-all-start = ((bf16[16,32,1024]{2,1,0:T(8,128)(2,1)}), bf16[16,32,1024]{2,1,0:T(8,128)(2,1)}, u32[]{:S(2)}, u32[]{:S(2)}) async-start(bf16[16,32,1024]{2,1,0:T(8,128)(2,1)} %broadcast_in_dim.2), calls=%async_computation | async-start | bytes 2097152 | tf_op jit(solution)/shard_map/all_to_all | solution.py:15
  12.4 0.0 copy-done.2
  12.5 0.0 copy-done.1
  12.5 26.9 %all-to-all-done = bf16[16,32,1024]{2,1,0:T(8,128)(2,1)} async-done(((bf16[16,32,1024]{2,1,0:T(8,128)(2,1)}), bf16[16,32,1024]{2,1,0:T(8,128)(2,1)}, u32[]{:S(2)}, u32[]{:S(2)}) %all-to-all-start) | async-done | bytes 1048608 | tf_op jit(solution)/shard_map/all_to_all | solution.py:15
  39.4 2.7 %reshape.31 = bf16[512,4,256,1]{2,1,0,3:T(4,128)(2,1)} reshape(bf16[16,32,1024]{2,1,0:T(8,128)(2,1)} %all-to-all-done) | data formatting | bytes 2097152 | tf_op jit(solution)/shard_map/reshape;reshape | solution.py:47
  42.1 3.5 %fusion.8 = bf16[8,3,512,256]{3,0,2,1:T(8,128)(2,1)S(1)} fusion(bf16[512,4,256,1]{2,1,0,3:T(4,128)(2,1)} %reshape.31, f32[8,3]{0,1:T(4,128)S(1)} %fusion.16, s32[8,3]{0,1:T(4,128)S(1)} %broadcast_subtract_fusion), kind=kOutput, calls=%fused_computation.10 | convolution fusion | flops 25166016 | bytes 7340224 | tf_op jit(solution)/shard_map/tkj,vjc->tkvc/dot_general | solution.py:48
  45.6 0.0 copy-done
  45.6 4.1 %fusion.3 = f32[8,512,256,1]{1,2,3,0:T(8,128)} fusion(bf16[8,3,256,256]{3,2,1,0:T(8,128)(2,1)S(1)} %copy-done, bf16[8,3,512,256]{3,0,2,1:T(8,128)(2,1)S(1)} %fusion.8), kind=kOutput, calls=%fused_computation.4 | convolution fusion | flops 1610612736 | bytes 13631488 | tf_op jit(solution)/shard_map/tkab,tkvb->vta/dot_general | solution.py:51
  49.7 136.0 %all-reduce.1 = bf16[512,2048]{0,1:T(8,128)(2,1)} all-reduce(f32[512,2048]{0,1:T(8,128)} %bitcast.34), channel_id=1, replica_groups=mesh['row'=16,'col'=32] {'col'}, use_global_device_ids=true, to_apply=%region_0.0 | all-reduce | flops 1048576 | bytes 6291456 | tf_op jit(solution)/shard_map/psum | solution.py:55
  185.7 3.4 %fusion.19 = f32[8,512,3,256]{3,1,2,0:T(8,128)S(1)} fusion(bf16[512,8,256,1]{0,2,3,1:T(8,128)(2,1)} %bitcast.35, bf16[8,3,256,256]{3,2,1,0:T(8,128)(2,1)S(1)} %copy-done), kind=kOutput, calls=%fused_computation.22 | convolution fusion | flops 1610612736 | bytes 17825792 | tf_op jit(solution)/shard_map/tkab,vta->tkvb/dot_general | solution.py:58
  189.1 12.5 %fusion.4 = f32[512,4,256]{2,1,0:T(4,128)} fusion(f32[8,512,3,256]{3,1,2,0:T(8,128)S(1)} %fusion.19, f32[8,3]{0,1:T(4,128)S(1)} %fusion.16, s32[8,3]{0,1:T(4,128)S(1)} %broadcast_subtract_fusion), kind=kOutput, calls=%fused_computation.5 | convolution fusion | flops 150995136 | bytes 14680256 | tf_op jit(solution)/shard_map/tkj,tkvb->vjb/dot_general | solution.py:61
  201.6 3.4 %reshape_reshape.7 = f32[16,32,1024]{2,1,0:T(8,128)} reshape(f32[512,4,256]{2,1,0:T(4,128)} %fusion.4) | data formatting | bytes 4194304 | tf_op jit(solution)/shard_map/reshape;reshape | solution.py:24
  205.0 53.2 %all_to_all.10 = f32[16,32,1024]{2,1,0:T(8,128)} all-to-all(f32[16,32,1024]{2,1,0:T(8,128)} %reshape_reshape.7), channel_id=1, replica_groups=mesh['row'=16,'col'=32] {'row'}, dimensions={0} | all-to-all | bytes 4194304 | tf_op jit(solution)/shard_map/all_to_all | solution.py:29
  258.1 2.4 reduce_sum.9
  (2 shorter events, 0.0 us)
Async XLA Ops:
  0.0 45.6 %copy-start = (bf16[8,3,256,256]{3,2,1,0:T(8,128)(2,1)S(1)}, bf16[8,3,256,256]{3,2,1,0:T(8,128)(2,1)}, u32[]{:S(2)}) copy-start(bf16[8,3,256,256]{3,2,1,0:T(8,128)(2,1)} %param.5) | copy-start | bytes 9437188
  0.0 12.4 %copy-start.2 = (s32[8,1]{0,1:T(1,128)S(1)}, s32[8,1]{0,1:T(1,128)}, u32[]{:S(2)}) copy-start(s32[8,1]{0,1:T(1,128)} %param.7) | copy-start | bytes 100
  0.0 12.5 %copy-start.1 = (s32[8,3]{0,1:T(4,128)S(1)}, s32[8,3]{0,1:T(4,128)}, u32[]{:S(2)}) copy-start(s32[8,3]{0,1:T(4,128)} %param.6) | copy-start | bytes 292
  2.2 37.3 %all-to-all-start = ((bf16[16,32,1024]{2,1,0:T(8,128)(2,1)}), bf16[16,32,1024]{2,1,0:T(8,128)(2,1)}, u32[]{:S(2)}, u32[]{:S(2)}) async-start(bf16[16,32,1024]{2,1,0:T(8,128)(2,1)} %broadcast_in_dim.2), calls=%async_computation | async-start | bytes 2097152 | tf_op jit(solution)/shard_map/all_to_all | solution.py:15
where the time goes:
time: 265 us; the launch traced here: 261 us
  blocking collectives  189 us (71%)
  waiting for transfers between devices  26.9 us (10%)
  matrix products  23.5 us (9%)
  starting transfers between devices  10.3 us (4%)
  local copies, waits for them, and re-layouts  8.17 us (3%)
    psum x1, blocking collectives, per_device(): rowvals = lax.psum(partial_all, 'col').astype(jnp.bfloat16)  136 us
    all_to_all x1, blocking collectives, sent_and_summed(): lax.all_to_all(tiles, axis, split_axis=0, concat_axis=0, tiled=True)  53.2 us
    all_to_all x1, waiting for transfers between devices, from_everyone(): return lax.all_to_all(copies, axis, split_axis=0, concat_axis=0, tiled=True)  26.9 us
    dot_general x1, matrix products, per_device(): jnp.einsum('tkj,tkvb->vjb', select_map, contrib, precision=lax.Precision....  12.5 us
    all_to_all x1, starting transfers between devices, from_everyone(): return lax.all_to_all(copies, axis, split_axis=0, concat_axis=0, tiled=True)  10.3 us
  transfers between devices with their start and end apart: 1, of which 1 were waited for; matrix products, arithmetic and copies ran while one was open for 0% of the time, Pallas kernels for 0%

commit v1 on v0

v1 whole, which is shorter than its diff:
```python
import functools

import jax
import jax.numpy as jnp
from jax import lax
from jax.experimental import pallas as pl
from jax.experimental.pallas import tpu as pltpu
from jax.sharding import PartitionSpec as P

BF16, F32 = jnp.bfloat16, jnp.float32
VMEM_BYTES = 40 * 1024 * 1024
LANES = 128
UNIT_BITS = 14


def swapped(shard, groups, axes):
    return lax.all_to_all(
        shard, axes, split_axis=0, concat_axis=0, axis_index_groups=groups, tiled=True
    )


def forward_kernel(own_tab, other_tab, vec_ref, own_ref, other_ref, out_ref, picked, total):
    step = pl.program_id(0)
    steps = total.shape[0]
    count, tile = picked.shape[1], picked.shape[2]
    per_core = picked.shape[0] // 2

    @pl.when(step == 0)
    def _():
        for col in range(2 * per_core):
            lo = (col % per_core) * tile
            block = vec_ref[:, col // per_core, :, lo : lo + tile]
            picked[col] = block.reshape(count, tile)

    acc = None
    for tab, ref in ((own_tab, own_ref), (other_tab, other_ref)):
        for slot in range(ref.shape[1]):
            col = tab[step, slot]
            values = picked[jnp.maximum(col, 0)]
            values = jnp.where(col >= 0, values, jnp.zeros_like(values))
            term = lax.dot_general(
                values, ref[0, slot], (((1,), (1,)), ((), ())), preferred_element_type=F32
            )
            acc = term if acc is None else acc + term
    total[step] = acc

    @pl.when(step == steps - 1)
    def _():
        most = jnp.zeros((count, tile), F32)
        for t in range(steps):
            most = jnp.maximum(most, jnp.abs(total[t]))
        most = jnp.max(most, axis=1, keepdims=True)
        power = jnp.floor(jnp.log2(jnp.maximum(most, 1e-30))) + 1.0
        unit = jnp.exp2(UNIT_BITS - power)
        parts, rows = out_ref.shape[0], out_ref.shape[1]
        for t in range(steps):
            code = jnp.floor(total[t] * unit + 0.5).astype(jnp.int32).astype(jnp.int16)
            out_ref[:, :, t * tile : (t + 1) * tile] = code.reshape(parts, rows, tile)
        power = jnp.broadcast_to(power, (count, LANES)).astype(jnp.int32).astype(jnp.int16)
        out_ref[:, :, steps * tile :] = power.reshape(parts, rows, LANES)


def forward(own_tab, other_tab, vecs, own, other):
    steps, slots, tile, _ = own.shape
    rows, _, part, width = vecs.shape
    count = rows * part
    smem = pl.BlockSpec(memory_space=pltpu.SMEM)
    tiles = pl.BlockSpec((1, slots, tile, tile), lambda t: (t, 0, 0, 0))
    shape = (rows, part, steps * tile + LANES)
    return pl.pallas_call(
        forward_kernel,
        grid=(steps,),
        in_specs=[smem, smem, pl.BlockSpec(vecs.shape, lambda t: (0, 0, 0, 0)), tiles, tiles],
        out_specs=pl.BlockSpec(shape, lambda t: (0, 0, 0)),
        out_shape=jax.ShapeDtypeStruct(shape, jnp.int16),
        scratch_shapes=[
            pltpu.VMEM((2 * width // tile, count, tile), BF16),
            pltpu.VMEM((steps, count, tile), F32),
        ],
        compiler_params=pltpu.CompilerParams(vmem_limit_bytes=VMEM_BYTES),
        cost_estimate=pl.CostEstimate(
            flops=4 * steps * slots * tile * tile * count,
            bytes_accessed=4 * own.size,
            transcendentals=0,
        ),
    )(own_tab, other_tab, vecs, own, other)


def settle_kernel(code_ref, out_ref):
    copies, _, width = out_ref.shape
    total = None
    for k in range(code_ref.shape[0]):
        power = code_ref[k, :, width:].astype(jnp.int32).astype(F32)
        unit = jnp.exp2(power[:, :1] - UNIT_BITS)
        term = code_ref[k, :, :width].astype(jnp.int32).astype(F32) * unit
        total = term if total is None else total + term
    value = total.astype(BF16)
    for k in range(copies):
        out_ref[k] = value


def settle(codes):
    copies, part, width = codes.shape
    return pl.pallas_call(
        settle_kernel,
        out_shape=jax.ShapeDtypeStruct((copies, part, width - LANES), BF16),
        compiler_params=pltpu.CompilerParams(vmem_limit_bytes=VMEM_BYTES),
    )(codes)


def backward_kernel(own_tab, other_tab, row_ref, own_ref, other_ref, out_ref, total):
    step = pl.program_id(0)
    cols, count, tile = total.shape
    per_core = cols // 2

    @pl.when(step == 0)
    def _():
        total[...] = jnp.zeros_like(total)

    values = row_ref[...].reshape(count, tile)
    for tab, ref in ((own_tab, own_ref), (other_tab, other_ref)):
        for slot in range(ref.shape[1]):
            col = tab[step, slot]
            term = jnp.dot(values, ref[0, slot], preferred_element_type=F32)
            place = jnp.maximum(col, 0)
            total[place] += jnp.where(col >= 0, term, jnp.zeros_like(term))

    @pl.when(step == pl.num_programs(0) - 1)
    def _():
        rows, _, part, _ = out_ref.shape
        for col in range(cols):
            lo = (col % per_core) * tile
            block = total[col].astype(BF16).reshape(rows, part, tile)
            out_ref[:, col // per_core, :, lo : lo + tile] = block


def backward(own_tab, other_tab, rowvals, own, other, shape):
    steps, slots, tile, _ = own.shape
    rows, part, _ = rowvals.shape
    count = rows * part
    smem = pl.BlockSpec(memory_space=pltpu.SMEM)
    tiles = pl.BlockSpec((1, slots, tile, tile), lambda t: (t, 0, 0, 0))
    return pl.pallas_call(
        backward_kernel,
        grid=(steps,),
        in_specs=[smem, smem, pl.BlockSpec((rows, part, tile), lambda t: (0, 0, t)), tiles, tiles],
        out_specs=pl.BlockSpec(shape, lambda t: (0, 0, 0, 0)),
        out_shape=jax.ShapeDtypeStruct(shape, BF16),
        scratch_shapes=[pltpu.VMEM((2 * shape[3] // tile, count, tile), F32)],
        compiler_params=pltpu.CompilerParams(vmem_limit_bytes=VMEM_BYTES),
        cost_estimate=pl.CostEstimate(
            flops=4 * steps * slots * tile * tile * count,
            bytes_accessed=4 * own.size,
            transcendentals=0,
        ),
    )(own_tab, other_tab, rowvals, own, other)


def per_device(n_row, n_col, vectors, factor_tiles, tile_columns, live_counts):
    _, slots, tile, _ = factor_tiles.shape
    chips = n_col // 2
    part = vectors.shape[0] // 2
    width = vectors.shape[1]
    col_tiles = width // tile
    pairs = [(c, c ^ 1) for c in range(n_col)]
    same_core = [[core + 2 * p for p in range(chips)] for core in range(2)]
    row_core = [
        [r * n_col + 2 * p + core for r in range(n_row) for core in range(2)] for p in range(chips)
    ]

    chip = lax.axis_index("col") // 2
    slot_index = lax.broadcasted_iota(jnp.int32, tile_columns.shape, 1)
    local = tile_columns - chip * (2 * col_tiles)
    own_tab = jnp.where(slot_index < live_counts, local, -1)
    other_tab = lax.ppermute(own_tab, "col", pairs)
    other_tiles = lax.ppermute(factor_tiles, "col", pairs)

    copies = jnp.broadcast_to(vectors, (n_row, 2 * part, width)).reshape(2 * n_row, part, width)
    gathered = swapped(copies, row_core, ("row", "col")).reshape(n_row, 2, part, width)

    codes = forward(own_tab, other_tab, gathered, factor_tiles, other_tiles)
    rowvals = settle(swapped(codes, same_core, "col"))
    rowvals = swapped(rowvals, same_core, "col")

    sums = backward(own_tab, other_tab, rowvals, factor_tiles, other_tiles, gathered.shape)
    sums = swapped(sums.reshape(2 * n_row, part, width), row_core, ("row", "col"))
    return sums.reshape(n_row, 2 * part, width).astype(F32).sum(axis=0)


def solution(mesh):
    in_specs = (P("row", "col"), P("row", "col", None, None), P("row", "col"), P("row", "col"))
    body = functools.partial(per_device, mesh.shape["row"], mesh.shape["col"])
    return jax.shard_map(
        body, mesh=mesh, in_specs=in_specs, out_specs=P("row", "col"), check_vma=False
    )
```

time: 265 us -> 167 us (0.63)
  blocking collectives: 189 us -> 106 us
  matrix products: 23.5 us -> 0 us
  Pallas kernels: 0 us -> 14.2 us
  local copies, waits for them, and re-layouts: 8.17 us -> 2.04 us
  starting transfers between devices: 10.3 us -> 15.8 us
    psum x1 -> x0, blocking collectives: 136 us -> none  [per_device(): rowvals = lax.psum(partial_all, 'col').astype(jnp.bfloat16)]
    all_to_all x1 -> x3, blocking collectives: 53.2 us -> 106 us  [swapped(): lax.all_to_all(shard, axes, split_axis=0, concat_axis=0, axis_index_group...]
    dot_general x4 -> x0, matrix products: 23.5 us -> none  [the longest x1 12.5 us: per_device(): jnp.einsum('tkj,tkvb->vjb', select_map, contrib, precision=lax.Precision....]
    pallas_call x0 -> x3, Pallas kernels: none -> 14.2 us  [the longest x1 7.31 us: forward(): pl.pallas_call(forward_kernel, grid=(steps,), in_specs=[smem, smem, pl.Bl...]
    ppermute x0 -> x2, starting transfers between devices: none -> 11.2 us  [the longest x1 9.04 us: per_device(): other_tiles = lax.ppermute(factor_tiles, 'col', pairs)]
    another operation x2 -> x0, local copies, waits for them, and re-layouts: 6 us -> none  [the longest x1 3.35 us: split_up(): return jnp.moveaxis(shard.reshape(*before, length, -1, *after), dim, 0)]
    all_to_all x1, starting transfers between devices: 10.3 us -> 4.52 us  [swapped(): lax.all_to_all(shard, axes, split_axis=0, concat_axis=0, axis_index_group...]
  transfers between devices with their start and end apart: 1 -> 3, of which waited for: 1 -> 2; matrix products, arithmetic and copies ran while one was open for 0% -> 1% of each run, Pallas kernels for 0% -> 0%
where the time goes in v1:
time: 167 us; the launch traced here: 164 us
  blocking collectives  106 us (63%)
  waiting for transfers between devices  25.4 us (15%)
  starting transfers between devices  15.8 us (9%)
  Pallas kernels  14.2 us (9%)
  local copies, waits for them, and re-layouts  2.04 us (1%)
    all_to_all x3, blocking collectives, swapped(): lax.all_to_all(shard, axes, split_axis=0, concat_axis=0, axis_index_group...  106 us
    all_to_all x1, waiting for transfers between devices, swapped(): lax.all_to_all(shard, axes, split_axis=0, concat_axis=0, axis_index_group...  24.6 us
    ppermute x1, starting transfers between devices, per_device(): other_tiles = lax.ppermute(factor_tiles, 'col', pairs)  9.04 us
    pallas_call x1, Pallas kernels, forward(): pl.pallas_call(forward_kernel, grid=(steps,), in_specs=[smem, smem, pl.Bl...  7.31 us
    pallas_call x1, Pallas kernels, backward(): pl.pallas_call(backward_kernel, grid=(steps,), in_specs=[smem, smem, pl.B...  6.59 us
    all_to_all x1, starting transfers between devices, swapped(): lax.all_to_all(shard, axes, split_axis=0, concat_axis=0, axis_index_group...  4.52 us
  transfers between devices with their start and end apart: 3, of which 2 were waited for; matrix products, arithmetic and copies ran while one was open for 1% of the time, Pallas kernels for 0%

profile of v1, /device:TPU:1, one launch (start us, length us, event | category | flops | bytes accessed | tf_op | source)
XLA Modules:
  0.0 164.5 jit_solution(2587036291866179497)
XLA Ops:
  0.0 0.0 copy-start
  0.0 0.0 copy-start.1
  0.0 0.0 copy-start.2
  0.0 9.0 %collective-permute-start.1 = (bf16[8,3,256,256]{3,2,1,0:T(8,128)(2,1)}, bf16[8,3,256,256]{3,2,1,0:T(8,128)(2,1)}, u32[]{:S(2)}, u32[]{:S(2)}) collective-permute-start(bf16[8,3,256,256]{3,2,1,0:T(8,128)(2,1)} %own_ref.3), channel_id=1, source_target_pairs={{0,1},{1,0},{2,3},{3,2},{4,5},{5,4},{6,7},{7,6},{8,9},{9,8},{10,11... | collective-permute-start | bytes 9437192 | tf_op jit(solution)/shard_map/ppermute | solution.py:176
  9.1 1.9 %broadcast_in_dim.8 = bf16[16,32,1024]{2,1,0:T(8,128)(2,1)} broadcast(bf16[32,1024]{1,0:T(8,128)(2,1)} %param.4), dimensions={1,2} | broadcast | bytes 1114112 | tf_op jit(solution)/shard_map/broadcast_in_dim | solution.py:178
  11.0 4.5 %all-to-all-start = ((bf16[32,16,1024]{2,1,0:T(8,128)(2,1)}), bf16[32,16,1024]{2,1,0:T(8,128)(2,1)}, u32[]{:S(2)}, u32[]{:S(2)}) async-start(bf16[32,16,1024]{2,1,0:T(8,128)(2,1)} %bitcast.9), calls=%async_computation | async-start | bytes 2097152 | tf_op jit(solution)/shard_map/all_to_all | solution.py:17
  15.5 0.0 copy-done.1
  15.6 0.1 copy.5
  15.6 0.0 copy-done.2
  15.6 0.1 subtract_select_fusion.own_tab
  15.7 2.2 %collective-permute-start = (s32[8,3]{1,0:T(8,128)S(1)}, s32[8,3]{1,0:T(8,128)S(1)}, u32[]{:S(2)}, u32[]{:S(2)}) collective-permute-start(s32[8,3]{1,0:T(8,128)S(1)} %subtract_select_fusion.own_tab), channel_id=1, source_target_pairs={{0,1},{1,0},{2,3},{3,2},{4,5},{5,4},{6,7},{7,6},{8,9},{9,8},{10,11... | collective-permute-start | bytes 296 | tf_op jit(solution)/shard_map/ppermute | solution.py:175
  17.9 0.8 collective-permute-done.other_tab
  18.8 24.6 %all-to-all-done = bf16[32,16,1024]{2,1,0:T(8,128)(2,1)} async-done(((bf16[32,16,1024]{2,1,0:T(8,128)(2,1)}), bf16[32,16,1024]{2,1,0:T(8,128)(2,1)}, u32[]{:S(2)}, u32[]{:S(2)}) %all-to-all-start) | async-done | bytes 1048608 | tf_op jit(solution)/shard_map/all_to_all | solution.py:17
  43.3 0.0 collective-permute-done.1.other_ref
  43.3 0.0 copy-done
  43.3 7.3 %shard_map.46 = s16[16,16,2176]{2,1,0:T(8,128)(2,1)S(1)} custom-call(s32[8,3]{1,0:T(8,128)S(1)} %subtract_select_fusion.own_tab, s32[8,3]{1,0:T(8,128)S(1)} %collective-permute-done.other_tab, bf16[16,2,16,1024]{3,2,1,0:T(8,128)(2,1)} %bitcast.2.vec_ref, bf16[8,3,256,256]{3,2,1,0:T(8,128)(2,1)S(1)} %copy-done, ...), custom_call_target="tpu_custom_call" | custom-call | flops 1610612736 | bytes 6291456 | tf_op jit(solution)/shard_map/pallas_call | solution.py:70
  50.6 37.6 %all_to_all.20.code_ref = s16[16,16,2176]{2,1,0:T(8,128)(2,1)S(1)} all-to-all(s16[16,16,2176]{2,1,0:T(8,128)(2,1)S(1)} %shard_map.46), channel_id=1, replica_groups={{0,2,4,6,8,10,12,14,16,18,20,22,24,26,28,30},{1,3,5,7,9,11,13,15,17,19,..., dimensions={0} | all-to-all | bytes 2228224 | tf_op jit(solution)/shard_map/all_to_all | solution.py:17
  88.2 0.3 shard_map.47
  88.6 28.7 %all_to_all.21.row_ref = bf16[16,16,2048]{2,1,0:T(8,128)(2,1)S(1)} all-to-all(bf16[16,16,2048]{2,1,0:T(8,128)(2,1)S(1)} %shard_map.47), channel_id=1, replica_groups={{0,2,4,6,8,10,12,14,16,18,20,22,24,26,28,30},{1,3,5,7,9,11,13,15,17,19,..., dimensions={0} | all-to-all | bytes 2097152 | tf_op jit(solution)/shard_map/all_to_all | solution.py:17
  117.3 6.6 %shard_map.48 = bf16[16,2,16,1024]{3,2,1,0:T(8,128)(2,1)S(1)} custom-call(s32[8,3]{1,0:T(8,128)S(1)} %subtract_select_fusion.own_tab, s32[8,3]{1,0:T(8,128)S(1)} %collective-permute-done.other_tab, bf16[16,16,2048]{2,1,0:T(8,128)(2,1)S(1)} %all_to_all.21.row_ref, bf16[8,3,256,256]{3,2,1,0:T(8,128)(2,1)S(1)} %copy-done, ...), custom_call_target="tpu_custom_call" | custom-call | flops 1610612736 | bytes 6291456 | tf_op jit(solution)/shard_map/pallas_call | solution.py:143
  123.9 39.7 %all_to_all.22 = bf16[32,16,1024]{2,1,0:T(8,128)(2,1)S(1)} all-to-all(bf16[32,16,1024]{2,1,0:T(8,128)(2,1)S(1)} %bitcast.8), channel_id=1, replica_groups={{0,1,32,33,64,65,96,97,128,129,160,161,192,193,224,225,256,257,288,289,..., dimensions={0} | all-to-all | bytes 2097152 | tf_op jit(solution)/shard_map/all_to_all | solution.py:17
  163.6 0.8 convert_reduce_fusion
Async XLA Ops:
  0.0 43.3 %copy-start = (bf16[8,3,256,256]{3,2,1,0:T(8,128)(2,1)S(1)}, bf16[8,3,256,256]{3,2,1,0:T(8,128)(2,1)}, u32[]{:S(2)}) copy-start(bf16[8,3,256,256]{3,2,1,0:T(8,128)(2,1)} %own_ref.3) | copy-start | bytes 9437188
  0.0 15.5 %copy-start.1 = (s32[8,3]{0,1:T(4,128)S(1)}, s32[8,3]{0,1:T(4,128)}, u32[]{:S(2)}) copy-start(s32[8,3]{0,1:T(4,128)} %param.6) | copy-start | bytes 292
  0.0 15.6 %copy-start.2 = (s32[8,1]{0,1:T(1,128)S(1)}, s32[8,1]{0,1:T(1,128)}, u32[]{:S(2)}) copy-start(s32[8,1]{0,1:T(1,128)} %param.7) | copy-start | bytes 100
  0.0 43.3 %collective-permute-start.1 = (bf16[8,3,256,256]{3,2,1,0:T(8,128)(2,1)}, bf16[8,3,256,256]{3,2,1,0:T(8,128)(2,1)}, u32[]{:S(2)}, u32[]{:S(2)}) collective-permute-start(bf16[8,3,256,256]{3,2,1,0:T(8,128)(2,1)} %own_ref.3), channel_id=1, source_target_pairs={{0,1},{1,0},{2,3},{3,2},{4,5},{5,4},{6,7},{7,6},{8,9},{9,8},{10,11... | collective-permute-start | bytes 9437192 | tf_op jit(solution)/shard_map/ppermute | solution.py:176
  11.0 32.3 %all-to-all-start = ((bf16[32,16,1024]{2,1,0:T(8,128)(2,1)}), bf16[32,16,1024]{2,1,0:T(8,128)(2,1)}, u32[]{:S(2)}, u32[]{:S(2)}) async-start(bf16[32,16,1024]{2,1,0:T(8,128)(2,1)} %bitcast.9), calls=%async_computation | async-start | bytes 2097152 | tf_op jit(solution)/shard_map/all_to_all | solution.py:17
  15.7 3.0 %collective-permute-start = (s32[8,3]{1,0:T(8,128)S(1)}, s32[8,3]{1,0:T(8,128)S(1)}, u32[]{:S(2)}, u32[]{:S(2)}) collective-permute-start(s32[8,3]{1,0:T(8,128)S(1)} %subtract_select_fusion.own_tab), channel_id=1, source_target_pairs={{0,1},{1,0},{2,3},{3,2},{4,5},{5,4},{6,7},{7,6},{8,9},{9,8},{10,11... | collective-permute-start | bytes 296 | tf_op jit(solution)/shard_map/ppermute | solution.py:175

commit v2 on v0

v2 whole, which is shorter than its diff:
```python
import functools

import jax
import jax.numpy as jnp
from jax import lax
from jax.experimental import pallas as pl
from jax.experimental.pallas import tpu as pltpu
from jax.sharding import PartitionSpec as P

BF16, F32 = jnp.bfloat16, jnp.float32
VMEM_BYTES = 24 * 1024 * 1024
LANES = 128
UNIT_BITS = 14
PIECES = 2


def swapped(shard, groups, axes):
    return lax.all_to_all(
        shard, axes, split_axis=0, concat_axis=0, axis_index_groups=groups, tiled=True
    )


SMEM = pl.BlockSpec(memory_space=pltpu.SMEM)
VMEM = pl.BlockSpec(memory_space=pltpu.VMEM)
ANY = pl.BlockSpec(memory_space=pl.ANY)


def params():
    return pltpu.CompilerParams(vmem_limit_bytes=VMEM_BYTES)


def cost(factor, count):
    slots = 2 * factor.shape[0] * factor.shape[1]
    tile = factor.shape[2]
    return pl.CostEstimate(
        flops=2 * slots * tile * tile * count,
        bytes_accessed=2 * slots * tile * tile,
        transcendentals=0,
    )


def spread_kernel(vec_ref, out_ref):
    for copy in range(out_ref.shape[0]):
        out_ref[copy] = vec_ref[...]


def spread(vectors, copies):
    return pl.pallas_call(
        spread_kernel,
        in_specs=[VMEM],
        out_specs=VMEM,
        out_shape=jax.ShapeDtypeStruct((copies, *vectors.shape), vectors.dtype),
        compiler_params=params(),
    )(vectors)


def fetches(sources, held, sems):
    depth = sources[0].shape[0]
    return [
        pltpu.make_async_copy(ref, held.at[k * depth : (k + 1) * depth], sems.at[k])
        for k, ref in enumerate(sources)
    ]


def forward_kernel(core_ref, own_tab, other_tab, vec_ref, own_ref, *refs):
    sources, (out_ref, picked, total, other_ref, sems) = refs[:PIECES], refs[PIECES:]
    steps, count, tile = total.shape
    per_core = picked.shape[0] // 2
    core = core_ref[0]
    copies = fetches(sources, other_ref, sems)
    for copy in copies:
        copy.start()
    for col in range(2 * per_core):
        lo = (col % per_core) * tile
        picked[col] = vec_ref[:, col // per_core, :, lo : lo + tile].reshape(count, tile)

    most = jnp.zeros((count, tile), F32)
    for tab, ref, side in ((own_tab, own_ref, core), (other_tab, other_ref, 1 - core)):
        if ref is other_ref:
            for copy in copies:
                copy.wait()
        for step in range(steps):
            acc = total[step] if ref is other_ref else None
            for slot in range(ref.shape[1]):
                col = tab[step, slot]
                values = picked[side * per_core + jnp.maximum(col, 0)]
                values = jnp.where(col >= 0, values, jnp.zeros_like(values))
                term = lax.dot_general(
                    values, ref[step, slot], (((1,), (1,)), ((), ())), preferred_element_type=F32
                )
                acc = term if acc is None else acc + term
            total[step] = acc
            if ref is other_ref:
                most = jnp.maximum(most, jnp.abs(acc))

    most = jnp.max(most, axis=1, keepdims=True)
    power = jnp.floor(jnp.log2(jnp.maximum(most, 1e-30))) + 1.0
    unit = jnp.exp2(UNIT_BITS - power)
    parts, rows = out_ref.shape[0], out_ref.shape[1]
    for step in range(steps):
        code = jnp.floor(total[step] * unit + 0.5).astype(jnp.int32).astype(jnp.int16)
        out_ref[:, :, step * tile : (step + 1) * tile] = code.reshape(parts, rows, tile)
    power = jnp.broadcast_to(power, (count, LANES)).astype(jnp.int32).astype(jnp.int16)
    out_ref[:, :, steps * tile :] = power.reshape(parts, rows, LANES)


def forward(core, own_tab, other_tab, vecs, own, other):
    steps, _, tile, _ = own.shape
    rows, _, part, width = vecs.shape
    count = rows * part
    return pl.pallas_call(
        forward_kernel,
        in_specs=[SMEM] * 3 + [VMEM] * 2 + [ANY] * PIECES,
        out_specs=VMEM,
        out_shape=jax.ShapeDtypeStruct((rows, part, steps * tile + LANES), jnp.int16),
        scratch_shapes=[
            pltpu.VMEM((2 * width // tile, count, tile), BF16),
            pltpu.VMEM((steps, count, tile), F32),
            pltpu.VMEM(own.shape, BF16),
            pltpu.SemaphoreType.DMA((PIECES,)),
        ],
        compiler_params=params(),
        cost_estimate=cost(own, count),
    )(core, own_tab, other_tab, vecs, own, *other)


def settle_kernel(code_ref, out_ref):
    copies, _, width = out_ref.shape
    total = None
    for k in range(code_ref.shape[0]):
        power = code_ref[k, :, width:].astype(jnp.int32).astype(F32)
        unit = jnp.exp2(power[:, :1] - UNIT_BITS)
        term = code_ref[k, :, :width].astype(jnp.int32).astype(F32) * unit
        total = term if total is None else total + term
    value = total.astype(BF16)
    for k in range(copies):
        out_ref[k] = value


def settle(codes):
    copies, part, width = codes.shape
    return pl.pallas_call(
        settle_kernel,
        in_specs=[VMEM],
        out_specs=VMEM,
        out_shape=jax.ShapeDtypeStruct((copies, part, width - LANES), BF16),
        compiler_params=params(),
    )(codes)


def backward_kernel(core_ref, own_tab, other_tab, row_ref, own_ref, *refs):
    sources, (out_ref, other_ref, sems) = refs[:PIECES], refs[PIECES:]
    rows, _, part, width = out_ref.shape
    steps, slots, tile, _ = own_ref.shape
    core = core_ref[0]
    copies = fetches(sources, other_ref, sems)
    for copy in copies:
        copy.start()
    for tab, ref, side in ((own_tab, own_ref, core), (other_tab, other_ref, 1 - core)):
        if ref is other_ref:
            for copy in copies:
                copy.wait()
        for col in range(width // tile):
            acc = None
            for step in range(steps):
                slot = jnp.int32(-1)
                for s in range(slots):
                    slot = jnp.where(tab[step, s] == col, s, slot)
                values = row_ref[:, :, step * tile : (step + 1) * tile].reshape(rows * part, tile)
                values = jnp.where(slot >= 0, values, jnp.zeros_like(values))
                term = jnp.dot(
                    values, ref[step, jnp.maximum(slot, 0)], preferred_element_type=F32
                )
                acc = term if acc is None else acc + term
            block = acc.astype(BF16).reshape(rows, part, tile)
            out_ref[:, side, :, col * tile : (col + 1) * tile] = block


def backward(core, own_tab, other_tab, rowvals, own, other, shape):
    return pl.pallas_call(
        backward_kernel,
        in_specs=[SMEM] * 3 + [VMEM] * 2 + [ANY] * PIECES,
        out_specs=VMEM,
        out_shape=jax.ShapeDtypeStruct(shape, BF16),
        scratch_shapes=[pltpu.VMEM(own.shape, BF16), pltpu.SemaphoreType.DMA((PIECES,))],
        compiler_params=params(),
        cost_estimate=cost(own, rowvals.shape[0] * rowvals.shape[1]),
    )(core, own_tab, other_tab, rowvals, own, *other)


def per_device(n_row, n_col, vectors, factor_tiles, tile_columns, live_counts):
    part = vectors.shape[0] // 2
    width = vectors.shape[1]
    col_tiles = width // factor_tiles.shape[2]
    chips = n_col // 2
    pairs = [(c, c ^ 1) for c in range(n_col)]
    same_core = [[core + 2 * p for p in range(chips)] for core in range(2)]
    row_core = [
        [r * n_col + 2 * p + core for r in range(n_row) for core in range(2)] for p in range(chips)
    ]

    col = lax.axis_index("col")
    core = (col & 1).reshape(1)
    copies = spread(vectors, n_row).reshape(2 * n_row, part, width)
    gathered = swapped(copies, row_core, ("row", "col")).reshape(n_row, 2, part, width)

    slot_index = lax.broadcasted_iota(jnp.int32, tile_columns.shape, 1)
    own_tab = jnp.where(slot_index < live_counts, tile_columns - col * col_tiles, -1)
    other_tab = lax.ppermute(own_tab, "col", pairs)
    other_tiles = []
    for piece in jnp.split(factor_tiles, PIECES):
        piece, other_tab = lax.optimization_barrier((piece, other_tab))
        other_tiles.append(lax.ppermute(piece, "col", pairs))

    codes = forward(core, own_tab, other_tab, gathered, factor_tiles, other_tiles)
    rowvals = settle(swapped(codes, same_core, "col"))
    rowvals = swapped(rowvals, same_core, "col")

    sums = backward(core, own_tab, other_tab, rowvals, factor_tiles, other_tiles, gathered.shape)
    sums = swapped(sums.reshape(2 * n_row, part, width), row_core, ("row", "col"))
    return sums.reshape(n_row, 2 * part, width).astype(F32).sum(axis=0)


def solution(mesh):
    in_specs = (P("row", "col"), P("row", "col", None, None), P("row", "col"), P("row", "col"))
    body = functools.partial(per_device, mesh.shape["row"], mesh.shape["col"])
    return jax.shard_map(
        body, mesh=mesh, in_specs=in_specs, out_specs=P("row", "col"), check_vma=False
    )
```

time: 265 us -> 161 us (0.61)
  blocking collectives: 189 us -> 106 us
  matrix products: 23.5 us -> 0 us
  Pallas kernels: 0 us -> 10.8 us
  waiting for transfers between devices: 26.9 us -> 19.1 us
  starting transfers between devices: 10.3 us -> 17.9 us
  local copies, waits for them, and re-layouts: 8.17 us -> 3.93 us
    psum x1 -> x0, blocking collectives: 136 us -> none  [per_device(): rowvals = lax.psum(partial_all, 'col').astype(jnp.bfloat16)]
    all_to_all x1 -> x3, blocking collectives: 53.2 us -> 106 us  [swapped(): lax.all_to_all(shard, axes, split_axis=0, concat_axis=0, axis_index_group...]
    dot_general x4 -> x0, matrix products: 23.5 us -> none  [the longest x1 12.5 us: per_device(): jnp.einsum('tkj,tkvb->vjb', select_map, contrib, precision=lax.Precision....]
    all_to_all x1, waiting for transfers between devices: 26.9 us -> 15.5 us  [swapped(): lax.all_to_all(shard, axes, split_axis=0, concat_axis=0, axis_index_group...]
    pallas_call x0 -> x4, Pallas kernels: none -> 10.8 us  [the longest x1 5.56 us: forward(): pl.pallas_call(forward_kernel, in_specs=[SMEM] * 3 + [VMEM] * 2 + [ANY] *...]
    ppermute x0 -> x3, starting transfers between devices: none -> 6.53 us  [the longest x2 4.32 us: per_device(): other_tiles.append(lax.ppermute(piece, 'col', pairs))]
    another operation x2 -> x0, local copies, waits for them, and re-layouts: 6 us -> none  [the longest x1 3.35 us: split_up(): return jnp.moveaxis(shard.reshape(*before, length, -1, *after), dim, 0)]
    ppermute x0 -> x3, waiting for transfers between devices: none -> 3.55 us  [the longest x2 3.55 us: per_device(): other_tiles.append(lax.ppermute(piece, 'col', pairs))]
  transfers between devices with their start and end apart: 1 -> 4, of which waited for: 1 -> 3; matrix products, arithmetic and copies ran while one was open for 0% -> 1% of each run, Pallas kernels for 0% -> 0%
where the time goes in v2:
time: 161 us; the launch traced here: 159 us
  blocking collectives  106 us (66%)
  waiting for transfers between devices  19.1 us (12%)
  starting transfers between devices  17.9 us (11%)
  Pallas kernels  10.8 us (7%)
  local copies, waits for them, and re-layouts  3.93 us (2%)
    all_to_all x3, blocking collectives, swapped(): lax.all_to_all(shard, axes, split_axis=0, concat_axis=0, axis_index_group...  106 us
    all_to_all x1, waiting for transfers between devices, swapped(): lax.all_to_all(shard, axes, split_axis=0, concat_axis=0, axis_index_group...  15.5 us
    all_to_all x1, starting transfers between devices, swapped(): lax.all_to_all(shard, axes, split_axis=0, concat_axis=0, axis_index_group...  11.4 us
    pallas_call x1, Pallas kernels, forward(): pl.pallas_call(forward_kernel, in_specs=[SMEM] * 3 + [VMEM] * 2 + [ANY] *...  5.56 us
    pallas_call x1, Pallas kernels, backward(): pl.pallas_call(backward_kernel, in_specs=[SMEM] * 3 + [VMEM] * 2 + [ANY]...  4.79 us
    ppermute x2, starting transfers between devices, per_device(): other_tiles.append(lax.ppermute(piece, 'col', pairs))  4.32 us
    ppermute x2, waiting for transfers between devices, per_device(): other_tiles.append(lax.ppermute(piece, 'col', pairs))  3.55 us
  transfers between devices with their start and end apart: 4, of which 3 were waited for; matrix products, arithmetic and copies ran while one was open for 1% of the time, Pallas kernels for 0%

profile of v2, /device:TPU:1, one launch (start us, length us, event | category | flops | bytes accessed | tf_op | source)
XLA Modules:
  0.0 158.7 jit_solution(11867120590524218694)
XLA Ops:
  0.0 0.0 copy-start.2
  0.0 0.8 copy-done.2
  0.8 0.0 copy-start.3
  0.8 0.0 copy-start.4
  0.8 0.0 copy-start
  0.8 0.1 shard_map.46
  0.9 0.0 copy-start.1
  0.9 1.0 copy-done.1
  1.9 11.4 %all-to-all-start = ((bf16[32,16,1024]{2,1,0:T(8,128)(2,1)}), bf16[32,16,1024]{2,1,0:T(8,128)(2,1)}, u32[]{:S(2)}, u32[]{:S(2)}) async-start(bf16[32,16,1024]{2,1,0:T(8,128)(2,1)} %bitcast.10), calls=%async_computation | async-start | bytes 2097152 | tf_op jit(solution)/shard_map/all_to_all | solution.py:18
  13.3 0.0 copy-done.3
  13.4 0.1 copy.5
  13.4 0.0 copy-done.4
  13.4 0.1 subtract_select_fusion.own_tab
  13.5 2.2 %collective-permute-start = (s32[8,3]{1,0:T(8,128)S(1)}, s32[8,3]{1,0:T(8,128)S(1)}, u32[]{:S(2)}, u32[]{:S(2)}) collective-permute-start(s32[8,3]{1,0:T(8,128)S(1)} %subtract_select_fusion.own_tab), channel_id=1, source_target_pairs={{0,1},{1,0},{2,3},{3,2},{4,5},{5,4},{6,7},{7,6},{8,9},{9,8},{10,11... | collective-permute-start | bytes 296 | tf_op jit(solution)/shard_map/ppermute | solution.py:209
  15.7 0.0 copy-done
  15.7 2.0 %fusion = (bf16[4,3,256,256]{3,2,1,0:T(8,128)(2,1)}, bf16[4,3,256,256]{3,2,1,0:T(8,128)(2,1)}) fusion(bf16[8,3,256,256]{3,2,1,0:T(8,128)(2,1)S(1)} %copy-done), kind=kLoop, calls=%fused_computation.3 | loop fusion | bytes 6291456 | tf_op jit(solution)/shard_map/split | solution.py:211
  17.7 0.0 collective-permute-done.other_tab
  17.7 2.1 %collective-permute-start.2 = (bf16[4,3,256,256]{3,2,1,0:T(8,128)(2,1)}, bf16[4,3,256,256]{3,2,1,0:T(8,128)(2,1)}, u32[]{:S(2)}, u32[]{:S(2)}) collective-permute-start(bf16[4,3,256,256]{3,2,1,0:T(8,128)(2,1)} %get-tuple-element.12), channel_id=1, source_target_pairs={{0,1},{1,0},{2,3},{3,2},{4,5},{5,4},{6,7},{7,6},{8,9},{9,8},{10,11... | collective-permute-start | bytes 4718600 | tf_op jit(solution)/shard_map/ppermute | solution.py:213
  19.8 2.2 %collective-permute-start.1 = (bf16[4,3,256,256]{3,2,1,0:T(8,128)(2,1)}, bf16[4,3,256,256]{3,2,1,0:T(8,128)(2,1)}, u32[]{:S(2)}, u32[]{:S(2)}) collective-permute-start(bf16[4,3,256,256]{3,2,1,0:T(8,128)(2,1)} %get-tuple-element.11), channel_id=1, source_target_pairs={{0,1},{1,0},{2,3},{3,2},{4,5},{5,4},{6,7},{7,6},{8,9},{9,8},{10,11... | collective-permute-start | bytes 4718600 | tf_op jit(solution)/shard_map/ppermute | solution.py:213
  22.1 1.3 collective-permute-done.2.refs_1_
  23.4 2.2 %collective-permute-done.1.refs_0_ = bf16[4,3,256,256]{3,2,1,0:T(8,128)(2,1)} collective-permute-done((bf16[4,3,256,256]{3,2,1,0:T(8,128)(2,1)}, bf16[4,3,256,256]{3,2,1,0:T(8,128)(2,1)}, u32[]{:S(2)}, u32[]{:S(2)}) %collective-permute-start.1) | collective-permute-done | bytes 1572896 | tf_op jit(solution)/shard_map/ppermute | solution.py:213
  25.6 15.5 %all-to-all-done = bf16[32,16,1024]{2,1,0:T(8,128)(2,1)} async-done(((bf16[32,16,1024]{2,1,0:T(8,128)(2,1)}), bf16[32,16,1024]{2,1,0:T(8,128)(2,1)}, u32[]{:S(2)}, u32[]{:S(2)}) %all-to-all-start) | async-done | bytes 1048608 | tf_op jit(solution)/shard_map/all_to_all | solution.py:18
  41.1 5.6 %shard_map.47 = s16[16,16,2176]{2,1,0:T(8,128)(2,1)S(1)} custom-call(s32[1]{0:T(128)} %bitcast.core_ref, s32[8,3]{1,0:T(8,128)S(1)} %subtract_select_fusion.own_tab, s32[8,3]{1,0:T(8,128)S(1)} %collective-permute-done.other_tab, bf16[16,2,16,1024]{3,2,1,0:T(8,128)(2,1)} %bitcast.3.vec_ref, bf16[8,3,256,256]{3,2,1,0:T(8,128)(2,1)S(1)} %copy-done, ...), custom_call_target="tpu_custom_call" | custom-call | flops 1610612736 | bytes 6291456 | tf_op jit(solution)/shard_map/pallas_call | solution.py:111
  46.7 37.6 %all_to_all.20.code_ref = s16[16,16,2176]{2,1,0:T(8,128)(2,1)S(1)} all-to-all(s16[16,16,2176]{2,1,0:T(8,128)(2,1)S(1)} %shard_map.47), channel_id=1, replica_groups={{0,2,4,6,8,10,12,14,16,18,20,22,24,26,28,30},{1,3,5,7,9,11,13,15,17,19,..., dimensions={0} | all-to-all | bytes 2228224 | tf_op jit(solution)/shard_map/all_to_all | solution.py:18
  84.3 0.3 shard_map.48
  84.6 28.7 %all_to_all.21.row_ref = bf16[16,16,2048]{2,1,0:T(8,128)(2,1)S(1)} all-to-all(bf16[16,16,2048]{2,1,0:T(8,128)(2,1)S(1)} %shard_map.48), channel_id=1, replica_groups={{0,2,4,6,8,10,12,14,16,18,20,22,24,26,28,30},{1,3,5,7,9,11,13,15,17,19,..., dimensions={0} | all-to-all | bytes 2097152 | tf_op jit(solution)/shard_map/all_to_all | solution.py:18
  113.3 4.8 %shard_map.49 = bf16[16,2,16,1024]{3,2,1,0:T(8,128)(2,1)S(1)} custom-call(s32[1]{0:T(128)} %bitcast.core_ref, s32[8,3]{1,0:T(8,128)S(1)} %subtract_select_fusion.own_tab, s32[8,3]{1,0:T(8,128)S(1)} %collective-permute-done.other_tab, bf16[16,16,2048]{2,1,0:T(8,128)(2,1)S(1)} %all_to_all.21.row_ref, bf16[8,3,256,256]{3,2,1,0:T(8,128)(2,1)S(1)} %copy-done, ...), custom_call_target="tpu_custom_call" | custom-call | flops 1610612736 | bytes 6291456 | tf_op jit(solution)/shard_map/pallas_call | solution.py:180
  118.1 39.7 %all_to_all.22 = bf16[32,16,1024]{2,1,0:T(8,128)(2,1)S(1)} all-to-all(bf16[32,16,1024]{2,1,0:T(8,128)(2,1)S(1)} %bitcast.9), channel_id=1, replica_groups={{0,1,32,33,64,65,96,97,128,129,160,161,192,193,224,225,256,257,288,289,..., dimensions={0} | all-to-all | bytes 2097152 | tf_op jit(solution)/shard_map/all_to_all | solution.py:18
  157.8 0.8 convert_reduce_fusion
Async XLA Ops:
  0.0 0.8 copy-start.2
  0.8 12.5 %copy-start.3 = (s32[8,3]{0,1:T(4,128)S(1)}, s32[8,3]{0,1:T(4,128)}, u32[]{:S(2)}) copy-start(s32[8,3]{0,1:T(4,128)} %param.6) | copy-start | bytes 292
  0.8 12.6 %copy-start.4 = (s32[8,1]{0,1:T(1,128)S(1)}, s32[8,1]{0,1:T(1,128)}, u32[]{:S(2)}) copy-start(s32[8,1]{0,1:T(1,128)} %param.7) | copy-start | bytes 100
  0.8 14.9 %copy-start = (bf16[8,3,256,256]{3,2,1,0:T(8,128)(2,1)S(1)}, bf16[8,3,256,256]{3,2,1,0:T(8,128)(2,1)}, u32[]{:S(2)}) copy-start(bf16[8,3,256,256]{3,2,1,0:T(8,128)(2,1)} %own_ref.3) | copy-start | bytes 9437188
  0.9 1.0 copy-start.1
  1.9 39.2 %all-to-all-start = ((bf16[32,16,1024]{2,1,0:T(8,128)(2,1)}), bf16[32,16,1024]{2,1,0:T(8,128)(2,1)}, u32[]{:S(2)}, u32[]{:S(2)}) async-start(bf16[32,16,1024]{2,1,0:T(8,128)(2,1)} %bitcast.10), calls=%async_computation | async-start | bytes 2097152 | tf_op jit(solution)/shard_map/all_to_all | solution.py:18
  13.5 4.2 %collective-permute-start = (s32[8,3]{1,0:T(8,128)S(1)}, s32[8,3]{1,0:T(8,128)S(1)}, u32[]{:S(2)}, u32[]{:S(2)}) collective-permute-start(s32[8,3]{1,0:T(8,128)S(1)} %subtract_select_fusion.own_tab), channel_id=1, source_target_pairs={{0,1},{1,0},{2,3},{3,2},{4,5},{5,4},{6,7},{7,6},{8,9},{9,8},{10,11... | collective-permute-start | bytes 296 | tf_op jit(solution)/shard_map/ppermute | solution.py:209
  17.7 5.6 %collective-permute-start.2 = (bf16[4,3,256,256]{3,2,1,0:T(8,128)(2,1)}, bf16[4,3,256,256]{3,2,1,0:T(8,128)(2,1)}, u32[]{:S(2)}, u32[]{:S(2)}) collective-permute-start(bf16[4,3,256,256]{3,2,1,0:T(8,128)(2,1)} %get-tuple-element.12), channel_id=1, source_target_pairs={{0,1},{1,0},{2,3},{3,2},{4,5},{5,4},{6,7},{7,6},{8,9},{9,8},{10,11... | collective-permute-start | bytes 4718600 | tf_op jit(solution)/shard_map/ppermute | solution.py:213
  19.8 5.8 %collective-permute-start.1 = (bf16[4,3,256,256]{3,2,1,0:T(8,128)(2,1)}, bf16[4,3,256,256]{3,2,1,0:T(8,128)(2,1)}, u32[]{:S(2)}, u32[]{:S(2)}) collective-permute-start(bf16[4,3,256,256]{3,2,1,0:T(8,128)(2,1)} %get-tuple-element.11), channel_id=1, source_target_pairs={{0,1},{1,0},{2,3},{3,2},{4,5},{5,4},{6,7},{7,6},{8,9},{9,8},{10,11... | collective-permute-start | bytes 4718600 | tf_op jit(solution)/shard_map/ppermute | solution.py:213

commit v3 on v2

v3 whole, which is shorter than its diff:
```python
import functools

import jax
import jax.numpy as jnp
from jax import lax
from jax.experimental import pallas as pl
from jax.experimental.pallas import tpu as pltpu
from jax.sharding import PartitionSpec as P

BF16, F32 = jnp.bfloat16, jnp.float32
VMEM_BYTES = 24 * 1024 * 1024
WIDE_BYTES = 48 * 1024 * 1024
LANES = 128
WIDEST_BYTES = 58 * 1024 * 1024
UNIT_BITS = 14
PIECES = 2


def swapped(shard, groups, axes):
    return lax.all_to_all(
        shard, axes, split_axis=0, concat_axis=0, axis_index_groups=groups, tiled=True
    )


SMEM = pl.BlockSpec(memory_space=pltpu.SMEM)
VMEM = pl.BlockSpec(memory_space=pltpu.VMEM)
ANY = pl.BlockSpec(memory_space=pl.ANY)


def params(limit=VMEM_BYTES):
    return pltpu.CompilerParams(vmem_limit_bytes=limit)


def cost(factor, count):
    return pl.CostEstimate(
        flops=2 * factor.size * count, bytes_accessed=2 * factor.size, transcendentals=0
    )


def spread_kernel(vec_ref, out_ref, sems):
    copies = [
        pltpu.make_async_copy(vec_ref, out_ref.at[k], sems.at[k]) for k in range(out_ref.shape[0])
    ]
    for copy in copies:
        copy.start()
    for copy in copies:
        copy.wait()


def spread(vectors, copies):
    return pl.pallas_call(
        spread_kernel,
        in_specs=[ANY],
        out_specs=ANY,
        out_shape=jax.ShapeDtypeStruct((copies, *vectors.shape), vectors.dtype),
        scratch_shapes=[pltpu.SemaphoreType.DMA((copies,))],
        compiler_params=params(WIDEST_BYTES),
    )(vectors)


def dense_kernel(own_tab, other_tab, own_ref, *refs):
    other_refs, out_ref = refs[:PIECES], refs[PIECES]
    step = pl.program_id(0)
    piece = step // (pl.num_programs(0) // PIECES)
    slots = own_ref.shape[1]
    cols = out_ref.shape[0] // 2
    for side, (tab, sources) in enumerate(((own_tab, [own_ref]), (other_tab, other_refs))):
        for col in range(cols):
            slot = jnp.int32(-1)
            for s in range(slots):
                slot = jnp.where(tab[step, s] == col, s, slot)
            block = jnp.zeros(out_ref.shape[1:], BF16)
            for k, ref in enumerate(sources):
                chosen = slot >= 0 if len(sources) == 1 else (slot >= 0) & (piece == k)
                block = jnp.where(chosen, ref[0, jnp.maximum(slot, 0)], block)
            out_ref[side * cols + col] = block


def dense(own_tab, other_tab, own, other, cols):
    steps, slots, tile, _ = own.shape
    depth = steps // PIECES
    tiles = [pl.BlockSpec((1, slots, tile, tile), lambda t: (t, 0, 0, 0))]
    for k in range(PIECES):
        place = lambda t, k=k: (jnp.clip(t - k * depth, 0, depth - 1), 0, 0, 0)
        tiles.append(pl.BlockSpec((1, slots, tile, tile), place))
    return pl.pallas_call(
        dense_kernel,
        grid=(steps,),
        in_specs=[SMEM, SMEM, *tiles],
        out_specs=pl.BlockSpec((2 * cols, tile, tile), lambda t: (0, t, 0)),
        out_shape=jax.ShapeDtypeStruct((2 * cols, steps * tile, tile), BF16),
        compiler_params=params(WIDE_BYTES),
        cost_estimate=pl.CostEstimate(flops=0, bytes_accessed=8 * own.size, transcendentals=0),
    )(own_tab, other_tab, own, *other)


def forward_kernel(core_ref, vec_ref, source_ref, out_ref, held, total, factor_ref, sems):
    rows, _, part, width = vec_ref.shape
    count = rows * part
    steps = total.shape[0]
    tile = total.shape[2]
    core = core_ref[0]
    strips = [pl.ds(step * tile, tile) for step in range(steps)]
    copies = [
        pltpu.make_async_copy(source_ref.at[:, strip], factor_ref.at[:, strip], sems.at[step])
        for step, strip in enumerate(strips)
    ]
    for copy in copies:
        copy.start()
    held[:, :width] = vec_ref[:, core].reshape(count, width)
    held[:, width:] = vec_ref[:, 1 - core].reshape(count, width)
    most = jnp.zeros((count, tile), F32)
    for step in range(steps):
        copies[step].wait()
        acc = None
        for col in range(factor_ref.shape[0]):
            term = lax.dot_general(
                held[:, col * tile : (col + 1) * tile],
                factor_ref[col, strips[step], :],
                (((1,), (1,)), ((), ())),
                preferred_element_type=F32,
            )
            acc = term if acc is None else acc + term
        total[step] = acc
        most = jnp.maximum(most, jnp.abs(acc))

    most = jnp.max(most, axis=1, keepdims=True)
    power = jnp.floor(jnp.log2(jnp.maximum(most, 1e-30))) + 1.0
    unit = jnp.exp2(UNIT_BITS - power)
    for step in range(steps):
        code = jnp.floor(total[step] * unit + 0.5).astype(jnp.int32).astype(jnp.int16)
        out_ref[:, :, step * tile : (step + 1) * tile] = code.reshape(rows, part, tile)
    power = jnp.broadcast_to(power, (count, LANES)).astype(jnp.int32).astype(jnp.int16)
    out_ref[:, :, steps * tile :] = power.reshape(rows, part, LANES)


def forward(core, vecs, factor):
    rows, _, part, width = vecs.shape
    count = rows * part
    _, height, tile = factor.shape
    return pl.pallas_call(
        forward_kernel,
        in_specs=[SMEM, VMEM, ANY],
        out_specs=VMEM,
        out_shape=jax.ShapeDtypeStruct((rows, part, height + LANES), jnp.int16),
        scratch_shapes=[
            pltpu.VMEM((count, 2 * width), BF16),
            pltpu.VMEM((height // tile, count, tile), F32),
            pltpu.VMEM(factor.shape, BF16),
            pltpu.SemaphoreType.DMA((height // tile,)),
        ],
        compiler_params=params(WIDE_BYTES),
        cost_estimate=cost(factor, count),
    )(core, vecs, factor)


def settle_kernel(code_ref, out_ref):
    copies, _, width = out_ref.shape
    total = None
    for k in range(code_ref.shape[0]):
        power = code_ref[k, :, width:].astype(jnp.int32).astype(F32)
        unit = jnp.exp2(power[:, :1] - UNIT_BITS)
        term = code_ref[k, :, :width].astype(jnp.int32).astype(F32) * unit
        total = term if total is None else total + term
    value = total.astype(BF16)
    for k in range(copies):
        out_ref[k] = value


def settle(codes):
    copies, part, width = codes.shape
    return pl.pallas_call(
        settle_kernel,
        in_specs=[VMEM],
        out_specs=VMEM,
        out_shape=jax.ShapeDtypeStruct((copies, part, width - LANES), BF16),
        compiler_params=params(),
    )(codes)


def backward_kernel(core_ref, row_ref, source_ref, out_ref, factor_ref, sems):
    rows, _, part, _ = out_ref.shape
    cols, _, tile = factor_ref.shape
    core = core_ref[0]
    copies = [
        pltpu.make_async_copy(source_ref.at[col], factor_ref.at[col], sems.at[col])
        for col in range(cols)
    ]
    for copy in copies:
        copy.start()
    values = row_ref[...].reshape(rows * part, row_ref.shape[2])
    for col in range(cols):
        copies[col].wait()
        place = core if col < cols // 2 else 1 - core
        lo = col % (cols // 2) * tile
        block = jnp.dot(values, factor_ref[col], preferred_element_type=F32)
        out_ref[:, place, :, lo : lo + tile] = block.astype(BF16).reshape(rows, part, tile)


def backward(core, rowvals, factor, shape):
    return pl.pallas_call(
        backward_kernel,
        in_specs=[SMEM, VMEM, ANY],
        out_specs=VMEM,
        out_shape=jax.ShapeDtypeStruct(shape, BF16),
        scratch_shapes=[
            pltpu.VMEM(factor.shape, BF16),
            pltpu.SemaphoreType.DMA((factor.shape[0],)),
        ],
        compiler_params=params(WIDE_BYTES),
        cost_estimate=cost(factor, rowvals.shape[0] * rowvals.shape[1]),
    )(core, rowvals, factor)


def per_device(n_row, n_col, vectors, factor_tiles, tile_columns, live_counts):
    part = vectors.shape[0] // 2
    width = vectors.shape[1]
    col_tiles = width // factor_tiles.shape[2]
    chips = n_col // 2
    pairs = [(c, c ^ 1) for c in range(n_col)]
    same_core = [[core + 2 * p for p in range(chips)] for core in range(2)]
    row_core = [
        [r * n_col + 2 * p + core for r in range(n_row) for core in range(2)] for p in range(chips)
    ]

    col = lax.axis_index("col")
    core = (col & 1).reshape(1)
    copies = spread(vectors, n_row).reshape(2 * n_row, part, width)
    gathered = swapped(copies, row_core, ("row", "col")).reshape(n_row, 2, part, width)

    slot_index = lax.broadcasted_iota(jnp.int32, tile_columns.shape, 1)
    own_tab = jnp.where(slot_index < live_counts, tile_columns - col * col_tiles, -1)
    other_tab = lax.ppermute(own_tab, "col", pairs)
    other_tiles = []
    for piece in jnp.split(factor_tiles, PIECES):
        piece, other_tab = lax.optimization_barrier((piece, other_tab))
        other_tiles.append(lax.ppermute(piece, "col", pairs))

    factor = dense(own_tab, other_tab, factor_tiles, other_tiles, col_tiles)
    codes = forward(core, gathered, factor)
    rowvals = settle(swapped(codes, same_core, "col"))
    rowvals = swapped(rowvals, same_core, "col")

    sums = backward(core, rowvals, factor, gathered.shape)
    sums = swapped(sums.reshape(2 * n_row, part, width), row_core, ("row", "col"))
    return sums.reshape(n_row, 2 * part, width).astype(F32).sum(axis=0)


def solution(mesh):
    in_specs = (P("row", "col"), P("row", "col", None, None), P("row", "col"), P("row", "col"))
    body = functools.partial(per_device, mesh.shape["row"], mesh.shape["col"])
    return jax.shard_map(
        body, mesh=mesh, in_specs=in_specs, out_specs=P("row", "col"), check_vma=False
    )
```

time: 161 us -> 196 us (1.22)
  Pallas kernels: 10.8 us -> 55.6 us
  waiting for transfers between devices: 19.1 us -> 9.38 us
    pallas_call x3 -> x4, Pallas kernels: 10.4 us -> 55.2 us  [the longest x1 33 us: spread(): pl.pallas_call(spread_kernel, in_specs=[ANY], out_specs=ANY, out_shape=ja...]
    all_to_all x1, waiting for transfers between devices: 15.5 us -> 5.82 us  [swapped(): lax.all_to_all(shard, axes, split_axis=0, concat_axis=0, axis_index_group...]
  transfers between devices with their start and end apart: 4 -> 4, of which waited for: 3 -> 3; matrix products, arithmetic and copies ran while one was open for 1% -> 2% of each run, Pallas kernels for 0% -> 4%
where the time goes in v3:
time: 196 us; the launch traced here: 194 us
  blocking collectives  106 us (54%)
  Pallas kernels  55.6 us (28%)
  starting transfers between devices  17.7 us (9%)
  waiting for transfers between devices  9.38 us (5%)
  local copies, waits for them, and re-layouts  3.93 us (2%)
    all_to_all x3, blocking collectives, swapped(): lax.all_to_all(shard, axes, split_axis=0, concat_axis=0, axis_index_group...  106 us
    pallas_call x1, Pallas kernels, spread(): pl.pallas_call(spread_kernel, in_specs=[ANY], out_specs=ANY, out_shape=ja...  33 us
    all_to_all x1, starting transfers between devices, swapped(): lax.all_to_all(shard, axes, split_axis=0, concat_axis=0, axis_index_group...  11.2 us
    pallas_call x1, Pallas kernels, dense(): pl.pallas_call(dense_kernel, grid=(steps,), in_specs=[SMEM, SMEM, *tiles]...  7.87 us
    pallas_call x1, Pallas kernels, forward(): pl.pallas_call(forward_kernel, in_specs=[SMEM, VMEM, ANY], out_specs=VMEM...  7.54 us
    pallas_call x1, Pallas kernels, backward(): pl.pallas_call(backward_kernel, in_specs=[SMEM, VMEM, ANY], out_specs=VME...  6.81 us
    all_to_all x1, waiting for transfers between devices, swapped(): lax.all_to_all(shard, axes, split_axis=0, concat_axis=0, axis_index_group...  5.82 us
    ppermute x2, starting transfers between devices, per_device(): other_tiles.append(lax.ppermute(piece, 'col', pairs))  4.32 us
  transfers between devices with their start and end apart: 4, of which 3 were waited for; matrix products, arithmetic and copies ran while one was open for 2% of the time, Pallas kernels for 4%

profile of v3, /device:TPU:1, one launch (start us, length us, event | category | flops | bytes accessed | tf_op | source)
XLA Modules:
  0.0 193.6 jit_solution(11706007587939682949)
XLA Ops:
  0.0 0.0 copy-start
  0.0 0.0 copy-start.1
  0.0 33.0 %shard_map.46 = bf16[16,32,1024]{2,1,0:T(8,128)(2,1)} custom-call(bf16[32,1024]{1,0:T(8,128)(2,1)} %vec_ref.1), custom_call_target="tpu_custom_call" | custom-call | tf_op jit(solution)/shard_map/pallas_call | solution.py:51
  33.0 11.2 %all-to-all-start = ((bf16[32,16,1024]{2,1,0:T(8,128)(2,1)}), bf16[32,16,1024]{2,1,0:T(8,128)(2,1)S(1)}, u32[]{:S(2)}, u32[]{:S(2)}) async-start(bf16[32,16,1024]{2,1,0:T(8,128)(2,1)} %bitcast.11), calls=%async_computation | async-start | bytes 2097152 | tf_op jit(solution)/shard_map/all_to_all | solution.py:20
  44.3 0.0 copy-done
  44.3 0.1 copy.5
  44.4 0.0 copy-done.1
  44.4 0.1 subtract_select_fusion.own_tab
  44.4 2.1 %collective-permute-start = (s32[8,3]{1,0:T(8,128)S(1)}, s32[8,3]{1,0:T(8,128)S(1)}, u32[]{:S(2)}, u32[]{:S(2)}) collective-permute-start(s32[8,3]{1,0:T(8,128)S(1)} %subtract_select_fusion.own_tab), channel_id=1, source_target_pairs={{0,1},{1,0},{2,3},{3,2},{4,5},{5,4},{6,7},{7,6},{8,9},{9,8},{10,11... | collective-permute-start | bytes 296 | tf_op jit(solution)/shard_map/ppermute | solution.py:233
  46.6 3.8 %fusion = (bf16[4,3,256,256]{3,2,1,0:T(8,128)(2,1)}, bf16[4,3,256,256]{3,2,1,0:T(8,128)(2,1)}) fusion(bf16[8,3,256,256]{3,2,1,0:T(8,128)(2,1)} %own_ref.1), kind=kLoop, calls=%fused_computation.3 | loop fusion | bytes 6291456 | tf_op jit(solution)/shard_map/split | solution.py:235
  50.4 0.0 collective-permute-done.other_tab
  50.4 2.2 %collective-permute-start.2 = (bf16[4,3,256,256]{3,2,1,0:T(8,128)(2,1)}, bf16[4,3,256,256]{3,2,1,0:T(8,128)(2,1)S(1)}, u32[]{:S(2)}, u32[]{:S(2)}) collective-permute-start(bf16[4,3,256,256]{3,2,1,0:T(8,128)(2,1)} %get-tuple-element.12), channel_id=1, source_target_pairs={{0,1},{1,0},{2,3},{3,2},{4,5},{5,4},{6,7},{7,6},{8,9},{9,8},{10,11... | collective-permute-start | bytes 4718600 | tf_op jit(solution)/shard_map/ppermute | solution.py:237
  52.6 2.1 %collective-permute-start.1 = (bf16[4,3,256,256]{3,2,1,0:T(8,128)(2,1)}, bf16[4,3,256,256]{3,2,1,0:T(8,128)(2,1)}, u32[]{:S(2)}, u32[]{:S(2)}) collective-permute-start(bf16[4,3,256,256]{3,2,1,0:T(8,128)(2,1)} %get-tuple-element.11), channel_id=1, source_target_pairs={{0,1},{1,0},{2,3},{3,2},{4,5},{5,4},{6,7},{7,6},{8,9},{9,8},{10,11... | collective-permute-start | bytes 4718600 | tf_op jit(solution)/shard_map/ppermute | solution.py:237
  54.7 1.2 collective-permute-done.2.refs_1_
  55.9 2.4 %collective-permute-done.1.refs_0_ = bf16[4,3,256,256]{3,2,1,0:T(8,128)(2,1)} collective-permute-done((bf16[4,3,256,256]{3,2,1,0:T(8,128)(2,1)}, bf16[4,3,256,256]{3,2,1,0:T(8,128)(2,1)}, u32[]{:S(2)}, u32[]{:S(2)}) %collective-permute-start.1) | collective-permute-done | bytes 1572896 | tf_op jit(solution)/shard_map/ppermute | solution.py:237
  58.3 7.9 %shard_map.47.source_ref = bf16[8,2048,256]{2,1,0:T(8,128)(2,1)} custom-call(s32[8,3]{1,0:T(8,128)S(1)} %subtract_select_fusion.own_tab, s32[8,3]{1,0:T(8,128)S(1)} %collective-permute-done.other_tab, bf16[8,3,256,256]{3,2,1,0:T(8,128)(2,1)} %own_ref.1, bf16[4,3,256,256]{3,2,1,0:T(8,128)(2,1)} %collective-permute-done.1.refs_0_, ...), custom_call_target="tpu_custom_call" | custom-call | bytes 12582912 | tf_op jit(solution)/shard_map/pallas_call | solution.py:86
  66.2 5.8 %all-to-all-done = bf16[32,16,1024]{2,1,0:T(8,128)(2,1)S(1)} async-done(((bf16[32,16,1024]{2,1,0:T(8,128)(2,1)}), bf16[32,16,1024]{2,1,0:T(8,128)(2,1)S(1)}, u32[]{:S(2)}, u32[]{:S(2)}) %all-to-all-start) | async-done | bytes 1048608 | tf_op jit(solution)/shard_map/all_to_all | solution.py:20
  72.0 7.5 %shard_map.48 = s16[16,16,2176]{2,1,0:T(8,128)(2,1)S(1)} custom-call(s32[1]{0:T(128)} %bitcast.core_ref, bf16[16,2,16,1024]{3,2,1,0:T(8,128)(2,1)S(1)} %bitcast.9, bf16[8,2048,256]{2,1,0:T(8,128)(2,1)} %shard_map.47.source_ref), custom_call_target="tpu_custom_call" | custom-call | flops 2147483648 | bytes 8388608 | tf_op jit(solution)/shard_map/pallas_call | solution.py:141
  79.5 37.6 %all_to_all.20.code_ref = s16[16,16,2176]{2,1,0:T(8,128)(2,1)S(1)} all-to-all(s16[16,16,2176]{2,1,0:T(8,128)(2,1)S(1)} %shard_map.48), channel_id=1, replica_groups={{0,2,4,6,8,10,12,14,16,18,20,22,24,26,28,30},{1,3,5,7,9,11,13,15,17,19,..., dimensions={0} | all-to-all | bytes 2228224 | tf_op jit(solution)/shard_map/all_to_all | solution.py:20
  117.1 0.3 shard_map.49
  117.5 28.7 %all_to_all.21.row_ref = bf16[16,16,2048]{2,1,0:T(8,128)(2,1)S(1)} all-to-all(bf16[16,16,2048]{2,1,0:T(8,128)(2,1)S(1)} %shard_map.49), channel_id=1, replica_groups={{0,2,4,6,8,10,12,14,16,18,20,22,24,26,28,30},{1,3,5,7,9,11,13,15,17,19,..., dimensions={0} | all-to-all | bytes 2097152 | tf_op jit(solution)/shard_map/all_to_all | solution.py:20
  146.2 6.8 %shard_map.50 = bf16[16,2,16,1024]{3,2,1,0:T(8,128)(2,1)S(1)} custom-call(s32[1]{0:T(128)} %bitcast.core_ref, bf16[16,16,2048]{2,1,0:T(8,128)(2,1)S(1)} %all_to_all.21.row_ref, bf16[8,2048,256]{2,1,0:T(8,128)(2,1)} %shard_map.47.source_ref), custom_call_target="tpu_custom_call" | custom-call | flops 2147483648 | bytes 8388608 | tf_op jit(solution)/shard_map/pallas_call | solution.py:201
  153.0 39.7 %all_to_all.22 = bf16[32,16,1024]{2,1,0:T(8,128)(2,1)S(1)} all-to-all(bf16[32,16,1024]{2,1,0:T(8,128)(2,1)S(1)} %bitcast.10), channel_id=1, replica_groups={{0,1,32,33,64,65,96,97,128,129,160,161,192,193,224,225,256,257,288,289,..., dimensions={0} | all-to-all | bytes 2097152 | tf_op jit(solution)/shard_map/all_to_all | solution.py:20
  192.7 0.8 convert_reduce_fusion
Async XLA Ops:
  0.0 44.3 %copy-start = (s32[8,3]{0,1:T(4,128)S(1)}, s32[8,3]{0,1:T(4,128)}, u32[]{:S(2)}) copy-start(s32[8,3]{0,1:T(4,128)} %param.6) | copy-start | bytes 292
  0.0 44.4 %copy-start.1 = (s32[8,1]{0,1:T(1,128)S(1)}, s32[8,1]{0,1:T(1,128)}, u32[]{:S(2)}) copy-start(s32[8,1]{0,1:T(1,128)} %param.7) | copy-start | bytes 100
  33.0 39.0 %all-to-all-start = ((bf16[32,16,1024]{2,1,0:T(8,128)(2,1)}), bf16[32,16,1024]{2,1,0:T(8,128)(2,1)S(1)}, u32[]{:S(2)}, u32[]{:S(2)}) async-start(bf16[32,16,1024]{2,1,0:T(8,128)(2,1)} %bitcast.11), calls=%async_computation | async-start | bytes 2097152 | tf_op jit(solution)/shard_map/all_to_all | solution.py:20
  44.4 6.0 %collective-permute-start = (s32[8,3]{1,0:T(8,128)S(1)}, s32[8,3]{1,0:T(8,128)S(1)}, u32[]{:S(2)}, u32[]{:S(2)}) collective-permute-start(s32[8,3]{1,0:T(8,128)S(1)} %subtract_select_fusion.own_tab), channel_id=1, source_target_pairs={{0,1},{1,0},{2,3},{3,2},{4,5},{5,4},{6,7},{7,6},{8,9},{9,8},{10,11... | collective-permute-start | bytes 296 | tf_op jit(solution)/shard_map/ppermute | solution.py:233
  50.4 5.5 %collective-permute-start.2 = (bf16[4,3,256,256]{3,2,1,0:T(8,128)(2,1)}, bf16[4,3,256,256]{3,2,1,0:T(8,128)(2,1)S(1)}, u32[]{:S(2)}, u32[]{:S(2)}) collective-permute-start(bf16[4,3,256,256]{3,2,1,0:T(8,128)(2,1)} %get-tuple-element.12), channel_id=1, source_target_pairs={{0,1},{1,0},{2,3},{3,2},{4,5},{5,4},{6,7},{7,6},{8,9},{9,8},{10,11... | collective-permute-start | bytes 4718600 | tf_op jit(solution)/shard_map/ppermute | solution.py:237
  52.6 5.7 %collective-permute-start.1 = (bf16[4,3,256,256]{3,2,1,0:T(8,128)(2,1)}, bf16[4,3,256,256]{3,2,1,0:T(8,128)(2,1)}, u32[]{:S(2)}, u32[]{:S(2)}) collective-permute-start(bf16[4,3,256,256]{3,2,1,0:T(8,128)(2,1)} %get-tuple-element.11), channel_id=1, source_target_pairs={{0,1},{1,0},{2,3},{3,2},{4,5},{5,4},{6,7},{7,6},{8,9},{9,8},{10,11... | collective-permute-start | bytes 4718600 | tf_op jit(solution)/shard_map/ppermute | solution.py:237

commit v4 on v2

--- a/solution.py
+++ b/solution.py
@@ -30,12 +30,8 @@
 
 
 def cost(factor, count):
-    slots = 2 * factor.shape[0] * factor.shape[1]
-    tile = factor.shape[2]
     return pl.CostEstimate(
-        flops=2 * slots * tile * tile * count,
-        bytes_accessed=2 * slots * tile * tile,
-        transcendentals=0,
+        flops=2 * factor.size * count, bytes_accessed=2 * factor.size, transcendentals=0
     )
 
 
@@ -120,8 +116,44 @@
             pltpu.SemaphoreType.DMA((PIECES,)),
         ],
         compiler_params=params(),
-        cost_estimate=cost(own, count),
+        cost_estimate=cost(own, 2 * count),
     )(core, own_tab, other_tab, vecs, own, *other)
+
+
+def dense_kernel(own_tab, other_tab, own_ref, *refs):
+    other_refs, out_ref = refs[:PIECES], refs[PIECES]
+    step = pl.program_id(0)
+    piece = step // (pl.num_programs(0) // PIECES)
+    slots = own_ref.shape[1]
+    cols = out_ref.shape[0] // 2
+    for side, (tab, sources) in enumerate(((own_tab, [own_ref]), (other_tab, other_refs))):
+        for col in range(cols):
+            slot = jnp.int32(-1)
+            for s in range(slots):
+                slot = jnp.where(tab[step, s] == col, s, slot)
+            block = jnp.zeros(out_ref.shape[1:], BF16)
+            for k, ref in enumerate(sources):
+                chosen = slot >= 0 if len(sources) == 1 else (slot >= 0) & (piece == k)
+                block = jnp.where(chosen, ref[0, jnp.maximum(slot, 0)], block)
+            out_ref[side * cols + col] = block
+
+
+def dense(own_tab, other_tab, own, other, cols):
+    steps, slots, tile, _ = own.shape
+    depth = steps // PIECES
+    tiles = [pl.BlockSpec((1, slots, tile, tile), lambda t: (t, 0, 0, 0))]
+    for k in range(PIECES):
+        place = lambda t, k=k: (jnp.clip(t - k * depth, 0, depth - 1), 0, 0, 0)
+        tiles.append(pl.BlockSpec((1, slots, tile, tile), place))
+    return pl.pallas_call(
+        dense_kernel,
+        grid=(steps,),
+        in_specs=[SMEM, SMEM, *tiles],
+        out_specs=pl.BlockSpec((2 * cols, tile, tile), lambda t: (0, t, 0)),
+        out_shape=jax.ShapeDtypeStruct((2 * cols, steps * tile, tile), BF16),
+        compiler_params=params(),
+        cost_estimate=pl.CostEstimate(flops=0, bytes_accessed=8 * own.size, transcendentals=0),
+    )(own_tab, other_tab, own, *other)
 
 
 def settle_kernel(code_ref, out_ref):
@@ -148,44 +180,27 @@
     )(codes)
 
 
-def backward_kernel(core_ref, own_tab, other_tab, row_ref, own_ref, *refs):
-    sources, (out_ref, other_ref, sems) = refs[:PIECES], refs[PIECES:]
-    rows, _, part, width = out_ref.shape
-    steps, slots, tile, _ = own_ref.shape
+def backward_kernel(core_ref, row_ref, factor_ref, out_ref):
+    rows, _, part, _ = out_ref.shape
+    cols, _, tile = factor_ref.shape
     core = core_ref[0]
-    copies = fetches(sources, other_ref, sems)
-    for copy in copies:
-        copy.start()
-    for tab, ref, side in ((own_tab, own_ref, core), (other_tab, other_ref, 1 - core)):
-        if ref is other_ref:
-            for copy in copies:
-                copy.wait()
-        for col in range(width // tile):
-            acc = None
-            for step in range(steps):
-                slot = jnp.int32(-1)
-                for s in range(slots):
-                    slot = jnp.where(tab[step, s] == col, s, slot)
-                values = row_ref[:, :, step * tile : (step + 1) * tile].reshape(rows * part, tile)
-                values = jnp.where(slot >= 0, values, jnp.zeros_like(values))
-                term = jnp.dot(
-                    values, ref[step, jnp.maximum(slot, 0)], preferred_element_type=F32
-                )
-                acc = term if acc is None else acc + term
-            block = acc.astype(BF16).reshape(rows, part, tile)
-            out_ref[:, side, :, col * tile : (col + 1) * tile] = block
-
-
-def backward(core, own_tab, other_tab, rowvals, own, other, shape):
+    values = row_ref[...].reshape(rows * part, row_ref.shape[2])
+    for col in range(cols):
+        place = core if col < cols // 2 else 1 - core
+        lo = col % (cols // 2) * tile
+        block = jnp.dot(values, factor_ref[col], preferred_element_type=F32)
+        out_ref[:, place, :, lo : lo + tile] = block.astype(BF16).reshape(rows, part, tile)
+
+
+def backward(core, rowvals, factor, shape):
     return pl.pallas_call(
         backward_kernel,
-        in_specs=[SMEM] * 3 + [VMEM] * 2 + [ANY] * PIECES,
+        in_specs=[SMEM, VMEM, VMEM],
         out_specs=VMEM,
         out_shape=jax.ShapeDtypeStruct(shape, BF16),
-        scratch_shapes=[pltpu.VMEM(own.shape, BF16), pltpu.SemaphoreType.DMA((PIECES,))],
-        compiler_params=params(),
-        cost_estimate=cost(own, rowvals.shape[0] * rowvals.shape[1]),
-    )(core, own_tab, other_tab, rowvals, own, *other)
+        compiler_params=params(),
+        cost_estimate=cost(factor, rowvals.shape[0] * rowvals.shape[1]),
+    )(core, rowvals, factor)
 
 
 def per_device(n_row, n_col, vectors, factor_tiles, tile_columns, live_counts):
@@ -212,11 +227,13 @@
         piece, other_tab = lax.optimization_barrier((piece, other_tab))
         other_tiles.append(lax.ppermute(piece, "col", pairs))
 
+    factor = dense(own_tab, other_tab, factor_tiles, other_tiles, col_tiles)
+    gathered, factor = lax.optimization_barrier((gathered, factor))
     codes = forward(core, own_tab, other_tab, gathered, factor_tiles, other_tiles)
     rowvals = settle(swapped(codes, same_core, "col"))
     rowvals = swapped(rowvals, same_core, "col")
 
-    sums = backward(core, own_tab, other_tab, rowvals, factor_tiles, other_tiles, gathered.shape)
+    sums = backward(core, rowvals, factor, gathered.shape)
     sums = swapped(sums.reshape(2 * n_row, part, width), row_core, ("row", "col"))
     return sums.reshape(n_row, 2 * part, width).astype(F32).sum(axis=0)
 

time: 161 us -> 159 us (0.988)
  waiting for transfers between devices: 19.1 us -> 10.5 us
  Pallas kernels: 10.8 us -> 14.3 us
  local copies, waits for them, and re-layouts: 3.93 us -> 7.13 us
    all_to_all x1, waiting for transfers between devices: 15.5 us -> 6.92 us  [swapped(): lax.all_to_all(shard, axes, split_axis=0, concat_axis=0, axis_index_group...]
    unnamed x11 -> x15, local copies, waits for them, and re-layouts: 1.94 us -> 5.2 us
    pallas_call x1 -> x2, Pallas kernels: 4.79 us -> 7.74 us  [the longest x1 5.41 us: dense(): pl.pallas_call(dense_kernel, grid=(steps,), in_specs=[SMEM, SMEM, *tiles]...]
  transfers between devices with their start and end apart: 4 -> 4, of which waited for: 3 -> 3; matrix products, arithmetic and copies ran while one was open for 1% -> 1% of each run, Pallas kernels for 0% -> 3%
where the time goes in v4:
time: 159 us; the launch traced here: 157 us
  blocking collectives  106 us (67%)
  starting transfers between devices  17.9 us (11%)
  Pallas kernels  14.3 us (9%)
  waiting for transfers between devices  10.5 us (7%)
  local copies, waits for them, and re-layouts  7.13 us (4%)
    all_to_all x3, blocking collectives, swapped(): lax.all_to_all(shard, axes, split_axis=0, concat_axis=0, axis_index_group...  106 us
    all_to_all x1, starting transfers between devices, swapped(): lax.all_to_all(shard, axes, split_axis=0, concat_axis=0, axis_index_group...  11.4 us
    all_to_all x1, waiting for transfers between devices, swapped(): lax.all_to_all(shard, axes, split_axis=0, concat_axis=0, axis_index_group...  6.92 us
    pallas_call x1, Pallas kernels, forward(): pl.pallas_call(forward_kernel, in_specs=[SMEM] * 3 + [VMEM] * 2 + [ANY] *...  6.14 us
    pallas_call x1, Pallas kernels, dense(): pl.pallas_call(dense_kernel, grid=(steps,), in_specs=[SMEM, SMEM, *tiles]...  5.41 us
    unnamed x15, local copies, waits for them, and re-layouts  5.2 us
    ppermute x2, starting transfers between devices, per_device(): other_tiles.append(lax.ppermute(piece, 'col', pairs))  4.32 us
    ppermute x2, waiting for transfers between devices, per_device(): other_tiles.append(lax.ppermute(piece, 'col', pairs))  3.55 us
  transfers between devices with their start and end apart: 4, of which 3 were waited for; matrix products, arithmetic and copies ran while one was open for 1% of the time, Pallas kernels for 3%

profile of v4, /device:TPU:1, one launch (start us, length us, event | category | flops | bytes accessed | tf_op | source)
XLA Modules:
  0.0 156.9 jit_solution(1935504340065289920)
XLA Ops:
  0.0 0.0 copy-start.4
  0.0 0.8 copy-done.4
  0.8 0.0 copy-start.5
  0.8 0.0 copy-start.6
  0.8 0.0 copy-start.2
  0.8 0.1 shard_map.46
  0.9 0.0 copy-start.3
  0.9 1.0 copy-done.3
  2.0 11.4 %all-to-all-start = ((bf16[32,16,1024]{2,1,0:T(8,128)(2,1)}), bf16[32,16,1024]{2,1,0:T(8,128)(2,1)}, u32[]{:S(2)}, u32[]{:S(2)}) async-start(bf16[32,16,1024]{2,1,0:T(8,128)(2,1)} %bitcast.9), calls=%async_computation | async-start | bytes 2097152 | tf_op jit(solution)/shard_map/all_to_all | solution.py:18
  13.4 0.0 copy-done.5
  13.4 0.1 copy.5
  13.5 0.0 copy-done.6
  13.5 0.1 subtract_select_fusion.own_tab
  13.6 2.2 %collective-permute-start = (s32[8,3]{1,0:T(8,128)S(1)}, s32[8,3]{1,0:T(8,128)S(1)}, u32[]{:S(2)}, u32[]{:S(2)}) collective-permute-start(s32[8,3]{1,0:T(8,128)S(1)} %subtract_select_fusion.own_tab), channel_id=1, source_target_pairs={{0,1},{1,0},{2,3},{3,2},{4,5},{5,4},{6,7},{7,6},{8,9},{9,8},{10,11... | collective-permute-start | bytes 296 | tf_op jit(solution)/shard_map/ppermute | solution.py:224
  15.8 0.0 copy-done.2
  15.8 1.9 %fusion = (bf16[4,3,256,256]{3,2,1,0:T(8,128)(2,1)}, bf16[4,3,256,256]{3,2,1,0:T(8,128)(2,1)}) fusion(bf16[8,3,256,256]{3,2,1,0:T(8,128)(2,1)S(1)} %copy-done.2), kind=kLoop, calls=%fused_computation.3 | loop fusion | bytes 6291456 | tf_op jit(solution)/shard_map/split | solution.py:226
  17.7 0.0 collective-permute-done.other_tab
  17.7 2.1 %collective-permute-start.2 = (bf16[4,3,256,256]{3,2,1,0:T(8,128)(2,1)}, bf16[4,3,256,256]{3,2,1,0:T(8,128)(2,1)}, u32[]{:S(2)}, u32[]{:S(2)}) collective-permute-start(bf16[4,3,256,256]{3,2,1,0:T(8,128)(2,1)} %get-tuple-element.14), channel_id=1, source_target_pairs={{0,1},{1,0},{2,3},{3,2},{4,5},{5,4},{6,7},{7,6},{8,9},{9,8},{10,11... | collective-permute-start | bytes 4718600 | tf_op jit(solution)/shard_map/ppermute | solution.py:228
  19.8 2.2 %collective-permute-start.1 = (bf16[4,3,256,256]{3,2,1,0:T(8,128)(2,1)}, bf16[4,3,256,256]{3,2,1,0:T(8,128)(2,1)}, u32[]{:S(2)}, u32[]{:S(2)}) collective-permute-start(bf16[4,3,256,256]{3,2,1,0:T(8,128)(2,1)} %get-tuple-element.13), channel_id=1, source_target_pairs={{0,1},{1,0},{2,3},{3,2},{4,5},{5,4},{6,7},{7,6},{8,9},{9,8},{10,11... | collective-permute-start | bytes 4718600 | tf_op jit(solution)/shard_map/ppermute | solution.py:228
  22.1 1.3 collective-permute-done.2.refs_1_
  23.4 2.2 %collective-permute-done.1.refs_0_ = bf16[4,3,256,256]{3,2,1,0:T(8,128)(2,1)} collective-permute-done((bf16[4,3,256,256]{3,2,1,0:T(8,128)(2,1)}, bf16[4,3,256,256]{3,2,1,0:T(8,128)(2,1)}, u32[]{:S(2)}, u32[]{:S(2)}) %collective-permute-start.1) | collective-permute-done | bytes 1572896 | tf_op jit(solution)/shard_map/ppermute | solution.py:228
  25.6 5.4 %shard_map.47.factor_ref = bf16[8,2048,256]{2,1,0:T(8,128)(2,1)S(1)} custom-call(s32[8,3]{1,0:T(8,128)S(1)} %subtract_select_fusion.own_tab, s32[8,3]{1,0:T(8,128)S(1)} %collective-permute-done.other_tab, bf16[8,3,256,256]{3,2,1,0:T(8,128)(2,1)S(1)} %copy-done.2, bf16[4,3,256,256]{3,2,1,0:T(8,128)(2,1)} %collective-permute-done.1.refs_0_, ...), custom_call_target="tpu_custom_call" | custom-call | bytes 12582912 | tf_op jit(solution)/shard_map/pallas_call | solution.py:148
  31.0 0.0 copy-start
  31.0 3.2 %copy-done = bf16[8,2048,256]{2,1,0:T(8,128)(2,1)} copy-done((bf16[8,2048,256]{2,1,0:T(8,128)(2,1)}, bf16[8,2048,256]{2,1,0:T(8,128)(2,1)S(1)}, u32[]{:S(2)}) %copy-start) | copy-done | bytes 8388632
  34.3 6.9 %all-to-all-done = bf16[32,16,1024]{2,1,0:T(8,128)(2,1)} async-done(((bf16[32,16,1024]{2,1,0:T(8,128)(2,1)}), bf16[32,16,1024]{2,1,0:T(8,128)(2,1)}, u32[]{:S(2)}, u32[]{:S(2)}) %all-to-all-start) | async-done | bytes 1048608 | tf_op jit(solution)/shard_map/all_to_all | solution.py:18
  41.2 0.0 copy-start.1
  41.2 6.1 %shard_map.48 = s16[16,16,2176]{2,1,0:T(8,128)(2,1)S(1)} custom-call(s32[1]{0:T(128)} %bitcast.core_ref, s32[8,3]{1,0:T(8,128)S(1)} %subtract_select_fusion.own_tab, s32[8,3]{1,0:T(8,128)S(1)} %collective-permute-done.other_tab, bf16[16,2,16,1024]{3,2,1,0:T(8,128)(2,1)} %bitcast.3.vec_ref, bf16[8,3,256,256]{3,2,1,0:T(8,128)(2,1)S(1)} %copy-done.2, ...), custom_call_target="tpu_custom_call" | custom-call | flops 1610612736 | bytes 3145728 | tf_op jit(solution)/shard_map/pallas_call | solution.py:107
  47.3 37.6 %all_to_all.20.code_ref = s16[16,16,2176]{2,1,0:T(8,128)(2,1)S(1)} all-to-all(s16[16,16,2176]{2,1,0:T(8,128)(2,1)S(1)} %shard_map.48), channel_id=1, replica_groups={{0,2,4,6,8,10,12,14,16,18,20,22,24,26,28,30},{1,3,5,7,9,11,13,15,17,19,..., dimensions={0} | all-to-all | bytes 2228224 | tf_op jit(solution)/shard_map/all_to_all | solution.py:18
  84.9 0.3 shard_map.49
  85.2 28.7 %all_to_all.21.row_ref = bf16[16,16,2048]{2,1,0:T(8,128)(2,1)S(1)} all-to-all(bf16[16,16,2048]{2,1,0:T(8,128)(2,1)S(1)} %shard_map.49), channel_id=1, replica_groups={{0,2,4,6,8,10,12,14,16,18,20,22,24,26,28,30},{1,3,5,7,9,11,13,15,17,19,..., dimensions={0} | all-to-all | bytes 2097152 | tf_op jit(solution)/shard_map/all_to_all | solution.py:18
  113.9 0.0 copy-done.1
  113.9 2.3 %shard_map.50 = bf16[16,2,16,1024]{3,2,1,0:T(8,128)(2,1)S(1)} custom-call(s32[1]{0:T(128)} %bitcast.core_ref, bf16[16,16,2048]{2,1,0:T(8,128)(2,1)S(1)} %all_to_all.21.row_ref, bf16[8,2048,256]{2,1,0:T(8,128)(2,1)S(1)} %copy-done.1), custom_call_target="tpu_custom_call" | custom-call | flops 2147483648 | bytes 8388608 | tf_op jit(solution)/shard_map/pallas_call | solution.py:196
  116.3 39.7 %all_to_all.22 = bf16[32,16,1024]{2,1,0:T(8,128)(2,1)S(1)} all-to-all(bf16[32,16,1024]{2,1,0:T(8,128)(2,1)S(1)} %bitcast.10), channel_id=1, replica_groups={{0,1,32,33,64,65,96,97,128,129,160,161,192,193,224,225,256,257,288,289,..., dimensions={0} | all-to-all | bytes 2097152 | tf_op jit(solution)/shard_map/all_to_all | solution.py:18
  156.0 0.8 convert_reduce_fusion
Async XLA Ops:
  0.0 0.8 copy-start.4
  0.8 12.6 %copy-start.5 = (s32[8,3]{0,1:T(4,128)S(1)}, s32[8,3]{0,1:T(4,128)}, u32[]{:S(2)}) copy-start(s32[8,3]{0,1:T(4,128)} %param.6) | copy-start | bytes 292
  0.8 12.6 %copy-start.6 = (s32[8,1]{0,1:T(1,128)S(1)}, s32[8,1]{0,1:T(1,128)}, u32[]{:S(2)}) copy-start(s32[8,1]{0,1:T(1,128)} %param.7) | copy-start | bytes 100
  0.8 14.9 %copy-start.2 = (bf16[8,3,256,256]{3,2,1,0:T(8,128)(2,1)S(1)}, bf16[8,3,256,256]{3,2,1,0:T(8,128)(2,1)}, u32[]{:S(2)}) copy-start(bf16[8,3,256,256]{3,2,1,0:T(8,128)(2,1)} %own_ref.3) | copy-start | bytes 9437188
  0.9 1.1 copy-start.3
  2.0 39.2 %all-to-all-start = ((bf16[32,16,1024]{2,1,0:T(8,128)(2,1)}), bf16[32,16,1024]{2,1,0:T(8,128)(2,1)}, u32[]{:S(2)}, u32[]{:S(2)}) async-start(bf16[32,16,1024]{2,1,0:T(8,128)(2,1)} %bitcast.9), calls=%async_computation | async-start | bytes 2097152 | tf_op jit(solution)/shard_map/all_to_all | solution.py:18
  13.6 4.2 %collective-permute-start = (s32[8,3]{1,0:T(8,128)S(1)}, s32[8,3]{1,0:T(8,128)S(1)}, u32[]{:S(2)}, u32[]{:S(2)}) collective-permute-start(s32[8,3]{1,0:T(8,128)S(1)} %subtract_select_fusion.own_tab), channel_id=1, source_target_pairs={{0,1},{1,0},{2,3},{3,2},{4,5},{5,4},{6,7},{7,6},{8,9},{9,8},{10,11... | collective-permute-start | bytes 296 | tf_op jit(solution)/shard_map/ppermute | solution.py:224
  17.7 5.6 %collective-permute-start.2 = (bf16[4,3,256,256]{3,2,1,0:T(8,128)(2,1)}, bf16[4,3,256,256]{3,2,1,0:T(8,128)(2,1)}, u32[]{:S(2)}, u32[]{:S(2)}) collective-permute-start(bf16[4,3,256,256]{3,2,1,0:T(8,128)(2,1)} %get-tuple-element.14), channel_id=1, source_target_pairs={{0,1},{1,0},{2,3},{3,2},{4,5},{5,4},{6,7},{7,6},{8,9},{9,8},{10,11... | collective-permute-start | bytes 4718600 | tf_op jit(solution)/shard_map/ppermute | solution.py:228
  19.8 5.8 %collective-permute-start.1 = (bf16[4,3,256,256]{3,2,1,0:T(8,128)(2,1)}, bf16[4,3,256,256]{3,2,1,0:T(8,128)(2,1)}, u32[]{:S(2)}, u32[]{:S(2)}) collective-permute-start(bf16[4,3,256,256]{3,2,1,0:T(8,128)(2,1)} %get-tuple-element.13), channel_id=1, source_target_pairs={{0,1},{1,0},{2,3},{3,2},{4,5},{5,4},{6,7},{7,6},{8,9},{9,8},{10,11... | collective-permute-start | bytes 4718600 | tf_op jit(solution)/shard_map/ppermute | solution.py:228
  31.0 3.2 %copy-start = (bf16[8,2048,256]{2,1,0:T(8,128)(2,1)}, bf16[8,2048,256]{2,1,0:T(8,128)(2,1)S(1)}, u32[]{:S(2)}) copy-start(bf16[8,2048,256]{2,1,0:T(8,128)(2,1)S(1)} %shard_map.47.factor_ref) | copy-start | bytes 25165828
  41.2 72.8 %copy-start.1 = (bf16[8,2048,256]{2,1,0:T(8,128)(2,1)S(1)}, bf16[8,2048,256]{2,1,0:T(8,128)(2,1)}, u32[]{:S(2)}) copy-start(bf16[8,2048,256]{2,1,0:T(8,128)(2,1)} %copy-done) | copy-start | bytes 25165828

commit v5 on v4

--- a/solution.py
+++ b/solution.py
@@ -58,46 +58,55 @@
     ]
 
 
-def forward_kernel(core_ref, own_tab, other_tab, vec_ref, own_ref, *refs):
-    sources, (out_ref, picked, total, other_ref, sems) = refs[:PIECES], refs[PIECES:]
+def forward_kernel(core_ref, own_tab, other_tab, vec_source, own_ref, *refs):
+    sources, (out_ref, vec_ref, picked, total, other_ref, sems) = refs[:PIECES], refs[PIECES:]
     steps, count, tile = total.shape
-    per_core = picked.shape[0] // 2
+    per_core = (picked.shape[0] - 1) // 2
     core = core_ref[0]
-    copies = fetches(sources, other_ref, sems)
+    copies = [
+        pltpu.make_async_copy(vec_source.at[:, side], vec_ref.at[k], sems.at[PIECES + k])
+        for k, side in enumerate((core, 1 - core))
+    ] + fetches(sources, other_ref, sems)
     for copy in copies:
         copy.start()
-    for col in range(2 * per_core):
-        lo = (col % per_core) * tile
-        picked[col] = vec_ref[:, col // per_core, :, lo : lo + tile].reshape(count, tile)
+    picked[2 * per_core] = jnp.zeros((count, tile), BF16)
 
     most = jnp.zeros((count, tile), F32)
-    for tab, ref, side in ((own_tab, own_ref, core), (other_tab, other_ref, 1 - core)):
-        if ref is other_ref:
-            for copy in copies:
-                copy.wait()
+    for side, (tab, ref) in enumerate(((own_tab, own_ref), (other_tab, other_ref))):
+        for copy in copies[1:] if side else copies[:1]:
+            copy.wait()
+        for col in range(per_core):
+            block = vec_ref[side, :, :, col * tile : (col + 1) * tile]
+            picked[side * per_core + col] = block.reshape(count, tile)
         for step in range(steps):
-            acc = total[step] if ref is other_ref else None
+            acc = total[step] if side else None
             for slot in range(ref.shape[1]):
                 col = tab[step, slot]
-                values = picked[side * per_core + jnp.maximum(col, 0)]
-                values = jnp.where(col >= 0, values, jnp.zeros_like(values))
+                values = picked[jnp.where(col >= 0, side * per_core + col, 2 * per_core)]
                 term = lax.dot_general(
                     values, ref[step, slot], (((1,), (1,)), ((), ())), preferred_element_type=F32
                 )
                 acc = term if acc is None else acc + term
             total[step] = acc
-            if ref is other_ref:
+            if side:
                 most = jnp.maximum(most, jnp.abs(acc))
 
     most = jnp.max(most, axis=1, keepdims=True)
     power = jnp.floor(jnp.log2(jnp.maximum(most, 1e-30))) + 1.0
     unit = jnp.exp2(UNIT_BITS - power)
-    parts, rows = out_ref.shape[0], out_ref.shape[1]
+    parts = out_ref.shape[0]
+    rows = count // parts
     for step in range(steps):
         code = jnp.floor(total[step] * unit + 0.5).astype(jnp.int32).astype(jnp.int16)
-        out_ref[:, :, step * tile : (step + 1) * tile] = code.reshape(parts, rows, tile)
-    power = jnp.broadcast_to(power, (count, LANES)).astype(jnp.int32).astype(jnp.int16)
-    out_ref[:, :, steps * tile :] = power.reshape(parts, rows, LANES)
+        for half in range(tile // LANES):
+            at = (step * (tile // LANES) + half) * rows
+            block = code[:, half * LANES : (half + 1) * LANES]
+            out_ref[:, at : at + rows] = block.reshape(parts, rows, LANES)
+    power = jnp.broadcast_to(power, (count, LANES)).reshape(parts, rows, LANES)
+    lane = lax.broadcasted_iota(jnp.int32, (parts, rows // 2, LANES), 2)
+    power = jnp.where(lane == 0, power[:, : rows // 2], power[:, rows // 2 :])
+    at = steps * (tile // LANES) * rows
+    out_ref[:, at:] = power.astype(jnp.int32).astype(jnp.int16)
 
 
 def forward(core, own_tab, other_tab, vecs, own, other):
@@ -106,14 +115,17 @@
     count = rows * part
     return pl.pallas_call(
         forward_kernel,
-        in_specs=[SMEM] * 3 + [VMEM] * 2 + [ANY] * PIECES,
-        out_specs=VMEM,
-        out_shape=jax.ShapeDtypeStruct((rows, part, steps * tile + LANES), jnp.int16),
+        in_specs=[SMEM] * 3 + [ANY, VMEM] + [ANY] * PIECES,
+        out_specs=VMEM,
+        out_shape=jax.ShapeDtypeStruct(
+            (rows, steps * (tile // LANES) * part + part // 2, LANES), jnp.int16
+        ),
         scratch_shapes=[
-            pltpu.VMEM((2 * width // tile, count, tile), BF16),
+            pltpu.VMEM((2, rows, part, width), BF16),
+            pltpu.VMEM((2 * width // tile + 1, count, tile), BF16),
             pltpu.VMEM((steps, count, tile), F32),
             pltpu.VMEM(own.shape, BF16),
-            pltpu.SemaphoreType.DMA((PIECES,)),
+            pltpu.SemaphoreType.DMA((PIECES + 2,)),
         ],
         compiler_params=params(),
         cost_estimate=cost(own, 2 * count),
@@ -157,25 +169,32 @@
 
 
 def settle_kernel(code_ref, out_ref):
-    copies, _, width = out_ref.shape
-    total = None
+    copies, rows, width = out_ref.shape
+    groups = width // LANES
+    units = []
     for k in range(code_ref.shape[0]):
-        power = code_ref[k, :, width:].astype(jnp.int32).astype(F32)
-        unit = jnp.exp2(power[:, :1] - UNIT_BITS)
-        term = code_ref[k, :, :width].astype(jnp.int32).astype(F32) * unit
-        total = term if total is None else total + term
-    value = total.astype(BF16)
-    for k in range(copies):
-        out_ref[k] = value
-
-
-def settle(codes):
-    copies, part, width = codes.shape
+        power = code_ref[k, groups * rows :].astype(jnp.int32).astype(F32)
+        power = jnp.concatenate([power[:, :1], power[:, 1:2]], axis=0)
+        units.append(jnp.exp2(power - UNIT_BITS))
+    for group in range(groups):
+        total = None
+        for k, unit in enumerate(units):
+            code = code_ref[k, group * rows : (group + 1) * rows]
+            term = code.astype(jnp.int32).astype(F32) * unit
+            total = term if total is None else total + term
+        value = total.astype(BF16)
+        for k in range(copies):
+            out_ref[k, :, group * LANES : (group + 1) * LANES] = value
+
+
+def settle(codes, part):
+    copies, height, _ = codes.shape
+    width = height // part * LANES
     return pl.pallas_call(
         settle_kernel,
         in_specs=[VMEM],
         out_specs=VMEM,
-        out_shape=jax.ShapeDtypeStruct((copies, part, width - LANES), BF16),
+        out_shape=jax.ShapeDtypeStruct((copies, part, width), BF16),
         compiler_params=params(),
     )(codes)
 
@@ -230,7 +249,7 @@
     factor = dense(own_tab, other_tab, factor_tiles, other_tiles, col_tiles)
     gathered, factor = lax.optimization_barrier((gathered, factor))
     codes = forward(core, own_tab, other_tab, gathered, factor_tiles, other_tiles)
-    rowvals = settle(swapped(codes, same_core, "col"))
+    rowvals = settle(swapped(codes, same_core, "col"), part)
     rowvals = swapped(rowvals, same_core, "col")
 
     sums = backward(core, rowvals, factor, gathered.shape)

time: 159 us -> 157 us (0.987)
  no operation moved by 1% of the time
where the time goes in v5:
time: 157 us; the launch traced here: 155 us
  blocking collectives  105 us (67%)
  starting transfers between devices  17.9 us (11%)
  Pallas kernels  13 us (8%)
  waiting for transfers between devices  10.5 us (7%)
  local copies, waits for them, and re-layouts  7.13 us (5%)
    all_to_all x3, blocking collectives, swapped(): lax.all_to_all(shard, axes, split_axis=0, concat_axis=0, axis_index_group...  105 us
    all_to_all x1, starting transfers between devices, swapped(): lax.all_to_all(shard, axes, split_axis=0, concat_axis=0, axis_index_group...  11.4 us
    all_to_all x1, waiting for transfers between devices, swapped(): lax.all_to_all(shard, axes, split_axis=0, concat_axis=0, axis_index_group...  6.92 us
    pallas_call x1, Pallas kernels, dense(): pl.pallas_call(dense_kernel, grid=(steps,), in_specs=[SMEM, SMEM, *tiles]...  5.41 us
    unnamed x15, local copies, waits for them, and re-layouts  5.2 us
    pallas_call x1, Pallas kernels, forward(): pl.pallas_call(forward_kernel, in_specs=[SMEM] * 3 + [ANY, VMEM] + [ANY]...  4.69 us
    ppermute x2, starting transfers between devices, per_device(): other_tiles.append(lax.ppermute(piece, 'col', pairs))  4.32 us
    ppermute x2, waiting for transfers between devices, per_device(): other_tiles.append(lax.ppermute(piece, 'col', pairs))  3.55 us
  transfers between devices with their start and end apart: 4, of which 3 were waited for; matrix products, arithmetic and copies ran while one was open for 1% of the time, Pallas kernels for 3%

profile of v5, /device:TPU:1, one launch (start us, length us, event | category | flops | bytes accessed | tf_op | source)
XLA Modules:
  0.0 154.9 jit_solution(3505553580230823747)
XLA Ops:
  0.0 0.0 copy-start.4
  0.0 0.8 copy-done.4
  0.8 0.0 copy-start.5
  0.8 0.0 copy-start.6
  0.8 0.0 copy-start.2
  0.8 0.1 shard_map.46
  0.9 0.0 copy-start.3
  0.9 1.0 copy-done.3
  2.0 11.4 %all-to-all-start = ((bf16[32,16,1024]{2,1,0:T(8,128)(2,1)}), bf16[32,16,1024]{2,1,0:T(8,128)(2,1)}, u32[]{:S(2)}, u32[]{:S(2)}) async-start(bf16[32,16,1024]{2,1,0:T(8,128)(2,1)} %bitcast.9), calls=%async_computation | async-start | bytes 2097152 | tf_op jit(solution)/shard_map/all_to_all | solution.py:18
  13.4 0.0 copy-done.5
  13.4 0.1 copy.5
  13.5 0.0 copy-done.6
  13.5 0.1 subtract_select_fusion.own_tab
  13.6 2.2 %collective-permute-start = (s32[8,3]{1,0:T(8,128)S(1)}, s32[8,3]{1,0:T(8,128)S(1)}, u32[]{:S(2)}, u32[]{:S(2)}) collective-permute-start(s32[8,3]{1,0:T(8,128)S(1)} %subtract_select_fusion.own_tab), channel_id=1, source_target_pairs={{0,1},{1,0},{2,3},{3,2},{4,5},{5,4},{6,7},{7,6},{8,9},{9,8},{10,11... | collective-permute-start | bytes 296 | tf_op jit(solution)/shard_map/ppermute | solution.py:243
  15.8 0.0 copy-done.2
  15.8 1.9 %fusion = (bf16[4,3,256,256]{3,2,1,0:T(8,128)(2,1)}, bf16[4,3,256,256]{3,2,1,0:T(8,128)(2,1)}) fusion(bf16[8,3,256,256]{3,2,1,0:T(8,128)(2,1)S(1)} %copy-done.2), kind=kLoop, calls=%fused_computation.3 | loop fusion | bytes 6291456 | tf_op jit(solution)/shard_map/split | solution.py:245
  17.7 0.0 collective-permute-done.other_tab
  17.7 2.1 %collective-permute-start.2 = (bf16[4,3,256,256]{3,2,1,0:T(8,128)(2,1)}, bf16[4,3,256,256]{3,2,1,0:T(8,128)(2,1)}, u32[]{:S(2)}, u32[]{:S(2)}) collective-permute-start(bf16[4,3,256,256]{3,2,1,0:T(8,128)(2,1)} %get-tuple-element.14), channel_id=1, source_target_pairs={{0,1},{1,0},{2,3},{3,2},{4,5},{5,4},{6,7},{7,6},{8,9},{9,8},{10,11... | collective-permute-start | bytes 4718600 | tf_op jit(solution)/shard_map/ppermute | solution.py:247
  19.8 2.2 %collective-permute-start.1 = (bf16[4,3,256,256]{3,2,1,0:T(8,128)(2,1)}, bf16[4,3,256,256]{3,2,1,0:T(8,128)(2,1)}, u32[]{:S(2)}, u32[]{:S(2)}) collective-permute-start(bf16[4,3,256,256]{3,2,1,0:T(8,128)(2,1)} %get-tuple-element.13), channel_id=1, source_target_pairs={{0,1},{1,0},{2,3},{3,2},{4,5},{5,4},{6,7},{7,6},{8,9},{9,8},{10,11... | collective-permute-start | bytes 4718600 | tf_op jit(solution)/shard_map/ppermute | solution.py:247
  22.1 1.3 collective-permute-done.2.refs_1_
  23.4 2.2 %collective-permute-done.1.refs_0_ = bf16[4,3,256,256]{3,2,1,0:T(8,128)(2,1)} collective-permute-done((bf16[4,3,256,256]{3,2,1,0:T(8,128)(2,1)}, bf16[4,3,256,256]{3,2,1,0:T(8,128)(2,1)}, u32[]{:S(2)}, u32[]{:S(2)}) %collective-permute-start.1) | collective-permute-done | bytes 1572896 | tf_op jit(solution)/shard_map/ppermute | solution.py:247
  25.6 5.4 %shard_map.47.factor_ref = bf16[8,2048,256]{2,1,0:T(8,128)(2,1)S(1)} custom-call(s32[8,3]{1,0:T(8,128)S(1)} %subtract_select_fusion.own_tab, s32[8,3]{1,0:T(8,128)S(1)} %collective-permute-done.other_tab, bf16[8,3,256,256]{3,2,1,0:T(8,128)(2,1)S(1)} %copy-done.2, bf16[4,3,256,256]{3,2,1,0:T(8,128)(2,1)} %collective-permute-done.1.refs_0_, ...), custom_call_target="tpu_custom_call" | custom-call | bytes 12582912 | tf_op jit(solution)/shard_map/pallas_call | solution.py:160
  31.0 0.0 copy-start
  31.0 3.2 %copy-done = bf16[8,2048,256]{2,1,0:T(8,128)(2,1)} copy-done((bf16[8,2048,256]{2,1,0:T(8,128)(2,1)}, bf16[8,2048,256]{2,1,0:T(8,128)(2,1)S(1)}, u32[]{:S(2)}) %copy-start) | copy-done | bytes 8388632
  34.3 6.9 %all-to-all-done = bf16[32,16,1024]{2,1,0:T(8,128)(2,1)} async-done(((bf16[32,16,1024]{2,1,0:T(8,128)(2,1)}), bf16[32,16,1024]{2,1,0:T(8,128)(2,1)}, u32[]{:S(2)}, u32[]{:S(2)}) %all-to-all-start) | async-done | bytes 1048608 | tf_op jit(solution)/shard_map/all_to_all | solution.py:18
  41.2 0.0 copy-start.1
  41.2 4.7 %shard_map.48 = s16[16,264,128]{2,1,0:T(8,128)(2,1)S(1)} custom-call(s32[1]{0:T(128)} %bitcast.core_ref, s32[8,3]{1,0:T(8,128)S(1)} %subtract_select_fusion.own_tab, s32[8,3]{1,0:T(8,128)S(1)} %collective-permute-done.other_tab, bf16[16,2,16,1024]{3,2,1,0:T(8,128)(2,1)} %bitcast.3.vec_source, bf16[8,3,256,256]{3,2,1,0:T(8,128)(2,1)S(1)} %copy-done.2, ...), custom_call_target="tpu_custom_call" | custom-call | flops 1610612736 | bytes 3145728 | tf_op jit(solution)/shard_map/pallas_call | solution.py:116
  45.9 37.0 %all_to_all.20.code_ref = s16[16,264,128]{2,1,0:T(8,128)(2,1)S(1)} all-to-all(s16[16,264,128]{2,1,0:T(8,128)(2,1)S(1)} %shard_map.48), channel_id=1, replica_groups={{0,2,4,6,8,10,12,14,16,18,20,22,24,26,28,30},{1,3,5,7,9,11,13,15,17,19,..., dimensions={0} | all-to-all | bytes 2162688 | tf_op jit(solution)/shard_map/all_to_all | solution.py:18
  82.9 0.5 shard_map.49
  83.4 28.8 %all_to_all.21.row_ref = bf16[16,16,2048]{2,1,0:T(8,128)(2,1)S(1)} all-to-all(bf16[16,16,2048]{2,1,0:T(8,128)(2,1)S(1)} %shard_map.49), channel_id=1, replica_groups={{0,2,4,6,8,10,12,14,16,18,20,22,24,26,28,30},{1,3,5,7,9,11,13,15,17,19,..., dimensions={0} | all-to-all | bytes 2097152 | tf_op jit(solution)/shard_map/all_to_all | solution.py:18
  112.2 0.0 copy-done.1
  112.2 2.3 %shard_map.50 = bf16[16,2,16,1024]{3,2,1,0:T(8,128)(2,1)S(1)} custom-call(s32[1]{0:T(128)} %bitcast.core_ref, bf16[16,16,2048]{2,1,0:T(8,128)(2,1)S(1)} %all_to_all.21.row_ref, bf16[8,2048,256]{2,1,0:T(8,128)(2,1)S(1)} %copy-done.1), custom_call_target="tpu_custom_call" | custom-call | flops 2147483648 | bytes 8388608 | tf_op jit(solution)/shard_map/pallas_call | solution.py:215
  114.5 39.5 %all_to_all.22 = bf16[32,16,1024]{2,1,0:T(8,128)(2,1)S(1)} all-to-all(bf16[32,16,1024]{2,1,0:T(8,128)(2,1)S(1)} %bitcast.10), channel_id=1, replica_groups={{0,1,32,33,64,65,96,97,128,129,160,161,192,193,224,225,256,257,288,289,..., dimensions={0} | all-to-all | bytes 2097152 | tf_op jit(solution)/shard_map/all_to_all | solution.py:18
  154.0 0.8 convert_reduce_fusion
Async XLA Ops:
  0.0 0.8 copy-start.4
  0.8 12.6 %copy-start.5 = (s32[8,3]{0,1:T(4,128)S(1)}, s32[8,3]{0,1:T(4,128)}, u32[]{:S(2)}) copy-start(s32[8,3]{0,1:T(4,128)} %param.6) | copy-start | bytes 292
  0.8 12.6 %copy-start.6 = (s32[8,1]{0,1:T(1,128)S(1)}, s32[8,1]{0,1:T(1,128)}, u32[]{:S(2)}) copy-start(s32[8,1]{0,1:T(1,128)} %param.7) | copy-start | bytes 100
  0.8 14.9 %copy-start.2 = (bf16[8,3,256,256]{3,2,1,0:T(8,128)(2,1)S(1)}, bf16[8,3,256,256]{3,2,1,0:T(8,128)(2,1)}, u32[]{:S(2)}) copy-start(bf16[8,3,256,256]{3,2,1,0:T(8,128)(2,1)} %own_ref.3) | copy-start | bytes 9437188
  0.9 1.1 copy-start.3
  2.0 39.2 %all-to-all-start = ((bf16[32,16,1024]{2,1,0:T(8,128)(2,1)}), bf16[32,16,1024]{2,1,0:T(8,128)(2,1)}, u32[]{:S(2)}, u32[]{:S(2)}) async-start(bf16[32,16,1024]{2,1,0:T(8,128)(2,1)} %bitcast.9), calls=%async_computation | async-start | bytes 2097152 | tf_op jit(solution)/shard_map/all_to_all | solution.py:18
  13.6 4.2 %collective-permute-start = (s32[8,3]{1,0:T(8,128)S(1)}, s32[8,3]{1,0:T(8,128)S(1)}, u32[]{:S(2)}, u32[]{:S(2)}) collective-permute-start(s32[8,3]{1,0:T(8,128)S(1)} %subtract_select_fusion.own_tab), channel_id=1, source_target_pairs={{0,1},{1,0},{2,3},{3,2},{4,5},{5,4},{6,7},{7,6},{8,9},{9,8},{10,11... | collective-permute-start | bytes 296 | tf_op jit(solution)/shard_map/ppermute | solution.py:243
  17.7 5.6 %collective-permute-start.2 = (bf16[4,3,256,256]{3,2,1,0:T(8,128)(2,1)}, bf16[4,3,256,256]{3,2,1,0:T(8,128)(2,1)}, u32[]{:S(2)}, u32[]{:S(2)}) collective-permute-start(bf16[4,3,256,256]{3,2,1,0:T(8,128)(2,1)} %get-tuple-element.14), channel_id=1, source_target_pairs={{0,1},{1,0},{2,3},{3,2},{4,5},{5,4},{6,7},{7,6},{8,9},{9,8},{10,11... | collective-permute-start | bytes 4718600 | tf_op jit(solution)/shard_map/ppermute | solution.py:247
  19.8 5.8 %collective-permute-start.1 = (bf16[4,3,256,256]{3,2,1,0:T(8,128)(2,1)}, bf16[4,3,256,256]{3,2,1,0:T(8,128)(2,1)}, u32[]{:S(2)}, u32[]{:S(2)}) collective-permute-start(bf16[4,3,256,256]{3,2,1,0:T(8,128)(2,1)} %get-tuple-element.13), channel_id=1, source_target_pairs={{0,1},{1,0},{2,3},{3,2},{4,5},{5,4},{6,7},{7,6},{8,9},{9,8},{10,11... | collective-permute-start | bytes 4718600 | tf_op jit(solution)/shard_map/ppermute | solution.py:247
  31.0 3.2 %copy-start = (bf16[8,2048,256]{2,1,0:T(8,128)(2,1)}, bf16[8,2048,256]{2,1,0:T(8,128)(2,1)S(1)}, u32[]{:S(2)}) copy-start(bf16[8,2048,256]{2,1,0:T(8,128)(2,1)S(1)} %shard_map.47.factor_ref) | copy-start | bytes 25165828
  41.2 71.0 %copy-start.1 = (bf16[8,2048,256]{2,1,0:T(8,128)(2,1)S(1)}, bf16[8,2048,256]{2,1,0:T(8,128)(2,1)}, u32[]{:S(2)}) copy-start(bf16[8,2048,256]{2,1,0:T(8,128)(2,1)} %copy-done) | copy-start | bytes 25165828

commit v6 on v5

--- a/solution.py
+++ b/solution.py
@@ -12,6 +12,8 @@
 LANES = 128
 UNIT_BITS = 14
 PIECES = 2
+ROW_ORDER = (14, 10, 8, 15, 9, 4, 13, 11, 12, 1, 0, 3, 2, 6, 5, 7)
+CHIP_ORDER = (3, 14, 7, 9, 13, 11, 4, 5, 12, 8, 1, 0, 15, 6, 2, 10)
 
 
 def swapped(shard, groups, axes):
@@ -228,9 +230,9 @@
     col_tiles = width // factor_tiles.shape[2]
     chips = n_col // 2
     pairs = [(c, c ^ 1) for c in range(n_col)]
-    same_core = [[core + 2 * p for p in range(chips)] for core in range(2)]
+    same_core = [[core + 2 * p for p in CHIP_ORDER] for core in range(2)]
     row_core = [
-        [r * n_col + 2 * p + core for r in range(n_row) for core in range(2)] for p in range(chips)
+        [r * n_col + 2 * p + core for r in ROW_ORDER for core in range(2)] for p in range(chips)
     ]
 
     col = lax.axis_index("col")

time: 157 us -> 153 us (0.975)
  waiting for transfers between devices: 10.5 us -> 6.76 us
  starting transfers between devices: 17.9 us -> 21.3 us
  blocking collectives: 105 us -> 102 us
    all_to_all x1, waiting for transfers between devices: 6.92 us -> 3.21 us  [swapped(): lax.all_to_all(shard, axes, split_axis=0, concat_axis=0, axis_index_group...]
    all_to_all x1, starting transfers between devices: 11.4 us -> 14.7 us  [swapped(): lax.all_to_all(shard, axes, split_axis=0, concat_axis=0, axis_index_group...]
    all_to_all x3, blocking collectives: 105 us -> 102 us  [swapped(): lax.all_to_all(shard, axes, split_axis=0, concat_axis=0, axis_index_group...]
  transfers between devices with their start and end apart: 4 -> 4, of which waited for: 3 -> 3; matrix products, arithmetic and copies ran while one was open for 1% -> 1% of each run, Pallas kernels for 3% -> 4%
where the time goes in v6:
time: 153 us; the launch traced here: 152 us
  blocking collectives  102 us (67%)
  starting transfers between devices  21.3 us (14%)
  Pallas kernels  13 us (8%)
  local copies, waits for them, and re-layouts  7.13 us (5%)
  waiting for transfers between devices  6.76 us (4%)
    all_to_all x3, blocking collectives, swapped(): lax.all_to_all(shard, axes, split_axis=0, concat_axis=0, axis_index_group...  102 us
    all_to_all x1, starting transfers between devices, swapped(): lax.all_to_all(shard, axes, split_axis=0, concat_axis=0, axis_index_group...  14.7 us
    pallas_call x1, Pallas kernels, dense(): pl.pallas_call(dense_kernel, grid=(steps,), in_specs=[SMEM, SMEM, *tiles]...  5.41 us
    unnamed x15, local copies, waits for them, and re-layouts  5.2 us
    pallas_call x1, Pallas kernels, forward(): pl.pallas_call(forward_kernel, in_specs=[SMEM] * 3 + [ANY, VMEM] + [ANY]...  4.69 us
    ppermute x2, starting transfers between devices, per_device(): other_tiles.append(lax.ppermute(piece, 'col', pairs))  4.32 us
    ppermute x2, waiting for transfers between devices, per_device(): other_tiles.append(lax.ppermute(piece, 'col', pairs))  3.55 us
    all_to_all x1, waiting for transfers between devices, swapped(): lax.all_to_all(shard, axes, split_axis=0, concat_axis=0, axis_index_group...  3.21 us
  transfers between devices with their start and end apart: 4, of which 3 were waited for; matrix products, arithmetic and copies ran while one was open for 1% of the time, Pallas kernels for 4%

profile of v6, /device:TPU:1, one launch (start us, length us, event | category | flops | bytes accessed | tf_op | source)
XLA Modules:
  0.0 151.5 jit_solution(12522525413109656048)
XLA Ops:
  0.0 0.0 copy-start.4
  0.0 0.8 copy-done.4
  0.8 0.0 copy-start.5
  0.8 0.0 copy-start.6
  0.8 0.0 copy-start.2
  0.8 0.1 shard_map.46
  0.9 0.0 copy-start.3
  0.9 1.0 copy-done.3
  2.0 14.7 %all-to-all-start = ((bf16[32,16,1024]{2,1,0:T(8,128)(2,1)}), bf16[32,16,1024]{2,1,0:T(8,128)(2,1)}, u32[]{:S(2)}, u32[]{:S(2)}) async-start(bf16[32,16,1024]{2,1,0:T(8,128)(2,1)} %bitcast.9), calls=%async_computation | async-start | bytes 2097152 | tf_op jit(solution)/shard_map/all_to_all | solution.py:20
  16.7 0.0 copy-done.5
  16.7 0.1 copy.5
  16.8 0.0 copy-done.6
  16.8 0.1 subtract_select_fusion.own_tab
  16.8 2.3 %collective-permute-start = (s32[8,3]{1,0:T(8,128)S(1)}, s32[8,3]{1,0:T(8,128)S(1)}, u32[]{:S(2)}, u32[]{:S(2)}) collective-permute-start(s32[8,3]{1,0:T(8,128)S(1)} %subtract_select_fusion.own_tab), channel_id=1, source_target_pairs={{0,1},{1,0},{2,3},{3,2},{4,5},{5,4},{6,7},{7,6},{8,9},{9,8},{10,11... | collective-permute-start | bytes 296 | tf_op jit(solution)/shard_map/ppermute | solution.py:245
  19.1 0.0 copy-done.2
  19.1 1.9 %fusion = (bf16[4,3,256,256]{3,2,1,0:T(8,128)(2,1)}, bf16[4,3,256,256]{3,2,1,0:T(8,128)(2,1)}) fusion(bf16[8,3,256,256]{3,2,1,0:T(8,128)(2,1)S(1)} %copy-done.2), kind=kLoop, calls=%fused_computation.3 | loop fusion | bytes 6291456 | tf_op jit(solution)/shard_map/split | solution.py:247
  21.1 0.0 collective-permute-done.other_tab
  21.1 2.0 %collective-permute-start.2 = (bf16[4,3,256,256]{3,2,1,0:T(8,128)(2,1)}, bf16[4,3,256,256]{3,2,1,0:T(8,128)(2,1)}, u32[]{:S(2)}, u32[]{:S(2)}) collective-permute-start(bf16[4,3,256,256]{3,2,1,0:T(8,128)(2,1)} %get-tuple-element.14), channel_id=1, source_target_pairs={{0,1},{1,0},{2,3},{3,2},{4,5},{5,4},{6,7},{7,6},{8,9},{9,8},{10,11... | collective-permute-start | bytes 4718600 | tf_op jit(solution)/shard_map/ppermute | solution.py:249
  23.1 2.3 %collective-permute-start.1 = (bf16[4,3,256,256]{3,2,1,0:T(8,128)(2,1)}, bf16[4,3,256,256]{3,2,1,0:T(8,128)(2,1)}, u32[]{:S(2)}, u32[]{:S(2)}) collective-permute-start(bf16[4,3,256,256]{3,2,1,0:T(8,128)(2,1)} %get-tuple-element.13), channel_id=1, source_target_pairs={{0,1},{1,0},{2,3},{3,2},{4,5},{5,4},{6,7},{7,6},{8,9},{9,8},{10,11... | collective-permute-start | bytes 4718600 | tf_op jit(solution)/shard_map/ppermute | solution.py:249
  25.4 1.3 collective-permute-done.2.refs_1_
  26.7 2.2 %collective-permute-done.1.refs_0_ = bf16[4,3,256,256]{3,2,1,0:T(8,128)(2,1)} collective-permute-done((bf16[4,3,256,256]{3,2,1,0:T(8,128)(2,1)}, bf16[4,3,256,256]{3,2,1,0:T(8,128)(2,1)}, u32[]{:S(2)}, u32[]{:S(2)}) %collective-permute-start.1) | collective-permute-done | bytes 1572896 | tf_op jit(solution)/shard_map/ppermute | solution.py:249
  28.9 5.4 %shard_map.47.factor_ref = bf16[8,2048,256]{2,1,0:T(8,128)(2,1)S(1)} custom-call(s32[8,3]{1,0:T(8,128)S(1)} %subtract_select_fusion.own_tab, s32[8,3]{1,0:T(8,128)S(1)} %collective-permute-done.other_tab, bf16[8,3,256,256]{3,2,1,0:T(8,128)(2,1)S(1)} %copy-done.2, bf16[4,3,256,256]{3,2,1,0:T(8,128)(2,1)} %collective-permute-done.1.refs_0_, ...), custom_call_target="tpu_custom_call" | custom-call | bytes 12582912 | tf_op jit(solution)/shard_map/pallas_call | solution.py:162
  34.4 0.0 copy-start
  34.4 3.2 %copy-done = bf16[8,2048,256]{2,1,0:T(8,128)(2,1)} copy-done((bf16[8,2048,256]{2,1,0:T(8,128)(2,1)}, bf16[8,2048,256]{2,1,0:T(8,128)(2,1)S(1)}, u32[]{:S(2)}) %copy-start) | copy-done | bytes 8388632
  37.6 3.2 %all-to-all-done = bf16[32,16,1024]{2,1,0:T(8,128)(2,1)} async-done(((bf16[32,16,1024]{2,1,0:T(8,128)(2,1)}), bf16[32,16,1024]{2,1,0:T(8,128)(2,1)}, u32[]{:S(2)}, u32[]{:S(2)}) %all-to-all-start) | async-done | bytes 1048608 | tf_op jit(solution)/shard_map/all_to_all | solution.py:20
  40.8 0.0 copy-start.1
  40.8 4.7 %shard_map.48 = s16[16,264,128]{2,1,0:T(8,128)(2,1)S(1)} custom-call(s32[1]{0:T(128)} %bitcast.core_ref, s32[8,3]{1,0:T(8,128)S(1)} %subtract_select_fusion.own_tab, s32[8,3]{1,0:T(8,128)S(1)} %collective-permute-done.other_tab, bf16[16,2,16,1024]{3,2,1,0:T(8,128)(2,1)} %bitcast.3.vec_source, bf16[8,3,256,256]{3,2,1,0:T(8,128)(2,1)S(1)} %copy-done.2, ...), custom_call_target="tpu_custom_call" | custom-call | flops 1610612736 | bytes 3145728 | tf_op jit(solution)/shard_map/pallas_call | solution.py:118
  45.5 37.9 %all_to_all.20.code_ref = s16[16,264,128]{2,1,0:T(8,128)(2,1)S(1)} all-to-all(s16[16,264,128]{2,1,0:T(8,128)(2,1)S(1)} %shard_map.48), channel_id=1, replica_groups={{6,28,14,18,26,22,8,10,24,16,2,0,30,12,4,20},{7,29,15,19,27,23,9,11,25,..., dimensions={0} | all-to-all | bytes 2162688 | tf_op jit(solution)/shard_map/all_to_all | solution.py:20
  83.4 0.5 shard_map.49
  83.9 27.5 %all_to_all.21.row_ref = bf16[16,16,2048]{2,1,0:T(8,128)(2,1)S(1)} all-to-all(bf16[16,16,2048]{2,1,0:T(8,128)(2,1)S(1)} %shard_map.49), channel_id=1, replica_groups={{6,28,14,18,26,22,8,10,24,16,2,0,30,12,4,20},{7,29,15,19,27,23,9,11,25,..., dimensions={0} | all-to-all | bytes 2097152 | tf_op jit(solution)/shard_map/all_to_all | solution.py:20
  111.4 0.0 copy-done.1
  111.4 2.3 %shard_map.50 = bf16[16,2,16,1024]{3,2,1,0:T(8,128)(2,1)S(1)} custom-call(s32[1]{0:T(128)} %bitcast.core_ref, bf16[16,16,2048]{2,1,0:T(8,128)(2,1)S(1)} %all_to_all.21.row_ref, bf16[8,2048,256]{2,1,0:T(8,128)(2,1)S(1)} %copy-done.1), custom_call_target="tpu_custom_call" | custom-call | flops 2147483648 | bytes 8388608 | tf_op jit(solution)/shard_map/pallas_call | solution.py:217
  113.7 37.0 %all_to_all.22 = bf16[32,16,1024]{2,1,0:T(8,128)(2,1)S(1)} all-to-all(bf16[32,16,1024]{2,1,0:T(8,128)(2,1)S(1)} %bitcast.10), channel_id=1, replica_groups={{448,449,320,321,256,257,480,481,288,289,128,129,416,417,352,353,384,38..., dimensions={0} | all-to-all | bytes 2097152 | tf_op jit(solution)/shard_map/all_to_all | solution.py:20
  150.7 0.8 convert_reduce_fusion
Async XLA Ops:
  0.0 0.8 copy-start.4
  0.8 15.8 %copy-start.5 = (s32[8,3]{0,1:T(4,128)S(1)}, s32[8,3]{0,1:T(4,128)}, u32[]{:S(2)}) copy-start(s32[8,3]{0,1:T(4,128)} %param.6) | copy-start | bytes 292
  0.8 15.9 %copy-start.6 = (s32[8,1]{0,1:T(1,128)S(1)}, s32[8,1]{0,1:T(1,128)}, u32[]{:S(2)}) copy-start(s32[8,1]{0,1:T(1,128)} %param.7) | copy-start | bytes 100
  0.8 18.3 %copy-start.2 = (bf16[8,3,256,256]{3,2,1,0:T(8,128)(2,1)S(1)}, bf16[8,3,256,256]{3,2,1,0:T(8,128)(2,1)}, u32[]{:S(2)}) copy-start(bf16[8,3,256,256]{3,2,1,0:T(8,128)(2,1)} %own_ref.3) | copy-start | bytes 9437188
  0.9 1.1 copy-start.3
  2.0 38.8 %all-to-all-start = ((bf16[32,16,1024]{2,1,0:T(8,128)(2,1)}), bf16[32,16,1024]{2,1,0:T(8,128)(2,1)}, u32[]{:S(2)}, u32[]{:S(2)}) async-start(bf16[32,16,1024]{2,1,0:T(8,128)(2,1)} %bitcast.9), calls=%async_computation | async-start | bytes 2097152 | tf_op jit(solution)/shard_map/all_to_all | solution.py:20
  16.8 4.2 %collective-permute-start = (s32[8,3]{1,0:T(8,128)S(1)}, s32[8,3]{1,0:T(8,128)S(1)}, u32[]{:S(2)}, u32[]{:S(2)}) collective-permute-start(s32[8,3]{1,0:T(8,128)S(1)} %subtract_select_fusion.own_tab), channel_id=1, source_target_pairs={{0,1},{1,0},{2,3},{3,2},{4,5},{5,4},{6,7},{7,6},{8,9},{9,8},{10,11... | collective-permute-start | bytes 296 | tf_op jit(solution)/shard_map/ppermute | solution.py:245
  21.1 5.6 %collective-permute-start.2 = (bf16[4,3,256,256]{3,2,1,0:T(8,128)(2,1)}, bf16[4,3,256,256]{3,2,1,0:T(8,128)(2,1)}, u32[]{:S(2)}, u32[]{:S(2)}) collective-permute-start(bf16[4,3,256,256]{3,2,1,0:T(8,128)(2,1)} %get-tuple-element.14), channel_id=1, source_target_pairs={{0,1},{1,0},{2,3},{3,2},{4,5},{5,4},{6,7},{7,6},{8,9},{9,8},{10,11... | collective-permute-start | bytes 4718600 | tf_op jit(solution)/shard_map/ppermute | solution.py:249
  23.1 5.8 %collective-permute-start.1 = (bf16[4,3,256,256]{3,2,1,0:T(8,128)(2,1)}, bf16[4,3,256,256]{3,2,1,0:T(8,128)(2,1)}, u32[]{:S(2)}, u32[]{:S(2)}) collective-permute-start(bf16[4,3,256,256]{3,2,1,0:T(8,128)(2,1)} %get-tuple-element.13), channel_id=1, source_target_pairs={{0,1},{1,0},{2,3},{3,2},{4,5},{5,4},{6,7},{7,6},{8,9},{9,8},{10,11... | collective-permute-start | bytes 4718600 | tf_op jit(solution)/shard_map/ppermute | solution.py:249
  34.4 3.2 %copy-start = (bf16[8,2048,256]{2,1,0:T(8,128)(2,1)}, bf16[8,2048,256]{2,1,0:T(8,128)(2,1)S(1)}, u32[]{:S(2)}) copy-start(bf16[8,2048,256]{2,1,0:T(8,128)(2,1)S(1)} %shard_map.47.factor_ref) | copy-start | bytes 25165828
  40.8 70.6 %copy-start.1 = (bf16[8,2048,256]{2,1,0:T(8,128)(2,1)S(1)}, bf16[8,2048,256]{2,1,0:T(8,128)(2,1)}, u32[]{:S(2)}) copy-start(bf16[8,2048,256]{2,1,0:T(8,128)(2,1)} %copy-done) | copy-start | bytes 25165828

commit v7 on v6

--- a/solution.py
+++ b/solution.py
@@ -13,7 +13,7 @@
 UNIT_BITS = 14
 PIECES = 2
 ROW_ORDER = (14, 10, 8, 15, 9, 4, 13, 11, 12, 1, 0, 3, 2, 6, 5, 7)
-CHIP_ORDER = (3, 14, 7, 9, 13, 11, 4, 5, 12, 8, 1, 0, 15, 6, 2, 10)
+CHIP_ORDERS = ((6, 15, 14, 8, 13, 10, 11, 12, 5, 1, 2, 7, 9, 0, 3, 4), (11, 5, 3, 7, 12, 2, 10, 8, 6, 4, 15, 0, 1, 13, 14, 9))
 
 
 def swapped(shard, groups, axes):
@@ -224,13 +224,30 @@
     )(core, rowvals, factor)
 
 
+def row_sum_kernel(part_ref, out_ref):
+    total = part_ref[0].astype(F32)
+    for k in range(1, part_ref.shape[0]):
+        total = total + part_ref[k].astype(F32)
+    out_ref[...] = total
+
+
+def row_sum(parts):
+    return pl.pallas_call(
+        row_sum_kernel,
+        in_specs=[VMEM],
+        out_specs=VMEM,
+        out_shape=jax.ShapeDtypeStruct(parts.shape[1:], F32),
+        compiler_params=params(),
+    )(parts)
+
+
 def per_device(n_row, n_col, vectors, factor_tiles, tile_columns, live_counts):
     part = vectors.shape[0] // 2
     width = vectors.shape[1]
     col_tiles = width // factor_tiles.shape[2]
     chips = n_col // 2
     pairs = [(c, c ^ 1) for c in range(n_col)]
-    same_core = [[core + 2 * p for p in CHIP_ORDER] for core in range(2)]
+    same_core = [[core + 2 * p for p in CHIP_ORDERS[core]] for core in range(2)]
     row_core = [
         [r * n_col + 2 * p + core for r in ROW_ORDER for core in range(2)] for p in range(chips)
     ]
@@ -256,7 +273,7 @@
 
     sums = backward(core, rowvals, factor, gathered.shape)
     sums = swapped(sums.reshape(2 * n_row, part, width), row_core, ("row", "col"))
-    return sums.reshape(n_row, 2 * part, width).astype(F32).sum(axis=0)
+    return row_sum(sums.reshape(n_row, 2 * part, width))
 
 
 def solution(mesh):

time: 153 us -> 152 us (level)
  no operation moved by 1% of the time
where the time goes in v7:
time: 152 us; the launch traced here: 151 us
  blocking collectives  102 us (67%)
  starting transfers between devices  21.3 us (14%)
  Pallas kernels  13.8 us (9%)
  local copies, waits for them, and re-layouts  7.12 us (5%)
  waiting for transfers between devices  6.78 us (4%)
    all_to_all x3, blocking collectives, swapped(): lax.all_to_all(shard, axes, split_axis=0, concat_axis=0, axis_index_group...  102 us
    all_to_all x1, starting transfers between devices, swapped(): lax.all_to_all(shard, axes, split_axis=0, concat_axis=0, axis_index_group...  14.7 us
    pallas_call x1, Pallas kernels, dense(): pl.pallas_call(dense_kernel, grid=(steps,), in_specs=[SMEM, SMEM, *tiles]...  5.41 us
    unnamed x15, local copies, waits for them, and re-layouts  5.19 us
    pallas_call x1, Pallas kernels, forward(): pl.pallas_call(forward_kernel, in_specs=[SMEM] * 3 + [ANY, VMEM] + [ANY]...  4.7 us
    ppermute x2, starting transfers between devices, per_device(): other_tiles.append(lax.ppermute(piece, 'col', pairs))  4.32 us
    ppermute x2, waiting for transfers between devices, per_device(): other_tiles.append(lax.ppermute(piece, 'col', pairs))  3.55 us
    all_to_all x1, waiting for transfers between devices, swapped(): lax.all_to_all(shard, axes, split_axis=0, concat_axis=0, axis_index_group...  3.22 us
  transfers between devices with their start and end apart: 4, of which 3 were waited for; matrix products, arithmetic and copies ran while one was open for 1% of the time, Pallas kernels for 4%

profile of v7, /device:TPU:1, one launch (start us, length us, event | category | flops | bytes accessed | tf_op | source)
XLA Modules:
  0.0 150.7 jit_solution(11731970471525237666)
XLA Ops:
  0.0 0.0 copy-start.4
  0.0 0.8 copy-done.4
  0.8 0.0 copy-start.5
  0.8 0.0 copy-start.6
  0.8 0.0 copy-start.2
  0.8 0.1 shard_map.46
  0.9 0.0 copy-start.3
  0.9 1.1 copy-done.3
  2.0 14.7 %all-to-all-start = ((bf16[32,16,1024]{2,1,0:T(8,128)(2,1)}), bf16[32,16,1024]{2,1,0:T(8,128)(2,1)}, u32[]{:S(2)}, u32[]{:S(2)}) async-start(bf16[32,16,1024]{2,1,0:T(8,128)(2,1)} %bitcast.6), calls=%async_computation | async-start | bytes 2097152 | tf_op jit(solution)/shard_map/all_to_all | solution.py:20
  16.7 0.0 copy-done.5
  16.7 0.1 copy.5
  16.8 0.0 copy-done.6
  16.8 0.1 subtract_select_fusion.own_tab
  16.8 2.3 %collective-permute-start = (s32[8,3]{1,0:T(8,128)S(1)}, s32[8,3]{1,0:T(8,128)S(1)}, u32[]{:S(2)}, u32[]{:S(2)}) collective-permute-start(s32[8,3]{1,0:T(8,128)S(1)} %subtract_select_fusion.own_tab), channel_id=1, source_target_pairs={{0,1},{1,0},{2,3},{3,2},{4,5},{5,4},{6,7},{7,6},{8,9},{9,8},{10,11... | collective-permute-start | bytes 296 | tf_op jit(solution)/shard_map/ppermute | solution.py:262
  19.1 0.0 copy-done.2
  19.1 1.9 %fusion = (bf16[4,3,256,256]{3,2,1,0:T(8,128)(2,1)}, bf16[4,3,256,256]{3,2,1,0:T(8,128)(2,1)}) fusion(bf16[8,3,256,256]{3,2,1,0:T(8,128)(2,1)S(1)} %copy-done.2), kind=kLoop, calls=%fused_computation.2 | loop fusion | bytes 6291456 | tf_op jit(solution)/shard_map/split | solution.py:264
  21.1 0.0 collective-permute-done.other_tab
  21.1 2.0 %collective-permute-start.2 = (bf16[4,3,256,256]{3,2,1,0:T(8,128)(2,1)}, bf16[4,3,256,256]{3,2,1,0:T(8,128)(2,1)}, u32[]{:S(2)}, u32[]{:S(2)}) collective-permute-start(bf16[4,3,256,256]{3,2,1,0:T(8,128)(2,1)} %get-tuple-element.14), channel_id=1, source_target_pairs={{0,1},{1,0},{2,3},{3,2},{4,5},{5,4},{6,7},{7,6},{8,9},{9,8},{10,11... | collective-permute-start | bytes 4718600 | tf_op jit(solution)/shard_map/ppermute | solution.py:266
  23.1 2.3 %collective-permute-start.1 = (bf16[4,3,256,256]{3,2,1,0:T(8,128)(2,1)}, bf16[4,3,256,256]{3,2,1,0:T(8,128)(2,1)}, u32[]{:S(2)}, u32[]{:S(2)}) collective-permute-start(bf16[4,3,256,256]{3,2,1,0:T(8,128)(2,1)} %get-tuple-element.13), channel_id=1, source_target_pairs={{0,1},{1,0},{2,3},{3,2},{4,5},{5,4},{6,7},{7,6},{8,9},{9,8},{10,11... | collective-permute-start | bytes 4718600 | tf_op jit(solution)/shard_map/ppermute | solution.py:266
  25.4 1.3 collective-permute-done.2.refs_1_
  26.7 2.2 %collective-permute-done.1.refs_0_ = bf16[4,3,256,256]{3,2,1,0:T(8,128)(2,1)} collective-permute-done((bf16[4,3,256,256]{3,2,1,0:T(8,128)(2,1)}, bf16[4,3,256,256]{3,2,1,0:T(8,128)(2,1)}, u32[]{:S(2)}, u32[]{:S(2)}) %collective-permute-start.1) | collective-permute-done | bytes 1572896 | tf_op jit(solution)/shard_map/ppermute | solution.py:266
  28.9 5.4 %shard_map.47.factor_ref = bf16[8,2048,256]{2,1,0:T(8,128)(2,1)S(1)} custom-call(s32[8,3]{1,0:T(8,128)S(1)} %subtract_select_fusion.own_tab, s32[8,3]{1,0:T(8,128)S(1)} %collective-permute-done.other_tab, bf16[8,3,256,256]{3,2,1,0:T(8,128)(2,1)S(1)} %copy-done.2, bf16[4,3,256,256]{3,2,1,0:T(8,128)(2,1)} %collective-permute-done.1.refs_0_, ...), custom_call_target="tpu_custom_call" | custom-call | bytes 12582912 | tf_op jit(solution)/shard_map/pallas_call | solution.py:162
  34.4 0.0 copy-start
  34.4 3.2 %copy-done = bf16[8,2048,256]{2,1,0:T(8,128)(2,1)} copy-done((bf16[8,2048,256]{2,1,0:T(8,128)(2,1)}, bf16[8,2048,256]{2,1,0:T(8,128)(2,1)S(1)}, u32[]{:S(2)}) %copy-start) | copy-done | bytes 8388632
  37.6 3.2 %all-to-all-done = bf16[32,16,1024]{2,1,0:T(8,128)(2,1)} async-done(((bf16[32,16,1024]{2,1,0:T(8,128)(2,1)}), bf16[32,16,1024]{2,1,0:T(8,128)(2,1)}, u32[]{:S(2)}, u32[]{:S(2)}) %all-to-all-start) | async-done | bytes 1048608 | tf_op jit(solution)/shard_map/all_to_all | solution.py:20
  40.8 0.0 copy-start.1
  40.8 4.7 %shard_map.48 = s16[16,264,128]{2,1,0:T(8,128)(2,1)S(1)} custom-call(s32[1]{0:T(128)} %bitcast.core_ref, s32[8,3]{1,0:T(8,128)S(1)} %subtract_select_fusion.own_tab, s32[8,3]{1,0:T(8,128)S(1)} %collective-permute-done.other_tab, bf16[16,2,16,1024]{3,2,1,0:T(8,128)(2,1)} %bitcast.3.vec_source, bf16[8,3,256,256]{3,2,1,0:T(8,128)(2,1)S(1)} %copy-done.2, ...), custom_call_target="tpu_custom_call" | custom-call | flops 1610612736 | bytes 3145728 | tf_op jit(solution)/shard_map/pallas_call | solution.py:118
  45.5 36.1 %all_to_all.20.code_ref = s16[16,264,128]{2,1,0:T(8,128)(2,1)S(1)} all-to-all(s16[16,264,128]{2,1,0:T(8,128)(2,1)S(1)} %shard_map.48), channel_id=1, replica_groups={{12,30,28,16,26,20,22,24,10,2,4,14,18,0,6,8},{23,11,7,15,25,5,21,17,13,..., dimensions={0} | all-to-all | bytes 2162688 | tf_op jit(solution)/shard_map/all_to_all | solution.py:20
  81.6 0.5 shard_map.49
  82.1 32.6 %all_to_all.21.row_ref = bf16[16,16,2048]{2,1,0:T(8,128)(2,1)S(1)} all-to-all(bf16[16,16,2048]{2,1,0:T(8,128)(2,1)S(1)} %shard_map.49), channel_id=1, replica_groups={{12,30,28,16,26,20,22,24,10,2,4,14,18,0,6,8},{23,11,7,15,25,5,21,17,13,..., dimensions={0} | all-to-all | bytes 2097152 | tf_op jit(solution)/shard_map/all_to_all | solution.py:20
  114.7 0.0 copy-done.1
  114.7 2.3 %shard_map.50 = bf16[16,2,16,1024]{3,2,1,0:T(8,128)(2,1)S(1)} custom-call(s32[1]{0:T(128)} %bitcast.core_ref, bf16[16,16,2048]{2,1,0:T(8,128)(2,1)S(1)} %all_to_all.21.row_ref, bf16[8,2048,256]{2,1,0:T(8,128)(2,1)S(1)} %copy-done.1), custom_call_target="tpu_custom_call" | custom-call | flops 2147483648 | bytes 8388608 | tf_op jit(solution)/shard_map/pallas_call | solution.py:217
  117.1 32.8 %all_to_all.22 = bf16[32,16,1024]{2,1,0:T(8,128)(2,1)S(1)} all-to-all(bf16[32,16,1024]{2,1,0:T(8,128)(2,1)S(1)} %bitcast.8), channel_id=1, replica_groups={{448,449,320,321,256,257,480,481,288,289,128,129,416,417,352,353,384,38..., dimensions={0} | all-to-all | bytes 2097152 | tf_op jit(solution)/shard_map/all_to_all | solution.py:20
  149.9 0.8 shard_map.51
Async XLA Ops:
  0.0 0.8 copy-start.4
  0.8 15.8 %copy-start.5 = (s32[8,3]{0,1:T(4,128)S(1)}, s32[8,3]{0,1:T(4,128)}, u32[]{:S(2)}) copy-start(s32[8,3]{0,1:T(4,128)} %param.6) | copy-start | bytes 292
  0.8 15.9 %copy-start.6 = (s32[8,1]{0,1:T(1,128)S(1)}, s32[8,1]{0,1:T(1,128)}, u32[]{:S(2)}) copy-start(s32[8,1]{0,1:T(1,128)} %param.7) | copy-start | bytes 100
  0.8 18.3 %copy-start.2 = (bf16[8,3,256,256]{3,2,1,0:T(8,128)(2,1)S(1)}, bf16[8,3,256,256]{3,2,1,0:T(8,128)(2,1)}, u32[]{:S(2)}) copy-start(bf16[8,3,256,256]{3,2,1,0:T(8,128)(2,1)} %own_ref.3) | copy-start | bytes 9437188
  0.9 1.1 copy-start.3
  2.0 38.8 %all-to-all-start = ((bf16[32,16,1024]{2,1,0:T(8,128)(2,1)}), bf16[32,16,1024]{2,1,0:T(8,128)(2,1)}, u32[]{:S(2)}, u32[]{:S(2)}) async-start(bf16[32,16,1024]{2,1,0:T(8,128)(2,1)} %bitcast.6), calls=%async_computation | async-start | bytes 2097152 | tf_op jit(solution)/shard_map/all_to_all | solution.py:20
  16.8 4.2 %collective-permute-start = (s32[8,3]{1,0:T(8,128)S(1)}, s32[8,3]{1,0:T(8,128)S(1)}, u32[]{:S(2)}, u32[]{:S(2)}) collective-permute-start(s32[8,3]{1,0:T(8,128)S(1)} %subtract_select_fusion.own_tab), channel_id=1, source_target_pairs={{0,1},{1,0},{2,3},{3,2},{4,5},{5,4},{6,7},{7,6},{8,9},{9,8},{10,11... | collective-permute-start | bytes 296 | tf_op jit(solution)/shard_map/ppermute | solution.py:262
  21.1 5.6 %collective-permute-start.2 = (bf16[4,3,256,256]{3,2,1,0:T(8,128)(2,1)}, bf16[4,3,256,256]{3,2,1,0:T(8,128)(2,1)}, u32[]{:S(2)}, u32[]{:S(2)}) collective-permute-start(bf16[4,3,256,256]{3,2,1,0:T(8,128)(2,1)} %get-tuple-element.14), channel_id=1, source_target_pairs={{0,1},{1,0},{2,3},{3,2},{4,5},{5,4},{6,7},{7,6},{8,9},{9,8},{10,11... | collective-permute-start | bytes 4718600 | tf_op jit(solution)/shard_map/ppermute | solution.py:266
  23.1 5.8 %collective-permute-start.1 = (bf16[4,3,256,256]{3,2,1,0:T(8,128)(2,1)}, bf16[4,3,256,256]{3,2,1,0:T(8,128)(2,1)}, u32[]{:S(2)}, u32[]{:S(2)}) collective-permute-start(bf16[4,3,256,256]{3,2,1,0:T(8,128)(2,1)} %get-tuple-element.13), channel_id=1, source_target_pairs={{0,1},{1,0},{2,3},{3,2},{4,5},{5,4},{6,7},{7,6},{8,9},{9,8},{10,11... | collective-permute-start | bytes 4718600 | tf_op jit(solution)/shard_map/ppermute | solution.py:266
  34.4 3.2 %copy-start = (bf16[8,2048,256]{2,1,0:T(8,128)(2,1)}, bf16[8,2048,256]{2,1,0:T(8,128)(2,1)S(1)}, u32[]{:S(2)}) copy-start(bf16[8,2048,256]{2,1,0:T(8,128)(2,1)S(1)} %shard_map.47.factor_ref) | copy-start | bytes 25165828
  40.8 73.9 %copy-start.1 = (bf16[8,2048,256]{2,1,0:T(8,128)(2,1)S(1)}, bf16[8,2048,256]{2,1,0:T(8,128)(2,1)}, u32[]{:S(2)}) copy-start(bf16[8,2048,256]{2,1,0:T(8,128)(2,1)} %copy-done) | copy-start | bytes 25165828

commit v8 on v7

--- a/solution.py
+++ b/solution.py
@@ -13,7 +13,7 @@
 UNIT_BITS = 14
 PIECES = 2
 ROW_ORDER = (14, 10, 8, 15, 9, 4, 13, 11, 12, 1, 0, 3, 2, 6, 5, 7)
-CHIP_ORDERS = ((6, 15, 14, 8, 13, 10, 11, 12, 5, 1, 2, 7, 9, 0, 3, 4), (11, 5, 3, 7, 12, 2, 10, 8, 6, 4, 15, 0, 1, 13, 14, 9))
+CHIP_ORDERS = ((3, 14, 7, 9, 13, 11, 4, 5, 12, 8, 1, 0, 15, 6, 2, 10), (14, 10, 8, 15, 9, 4, 13, 11, 12, 1, 0, 3, 2, 6, 5, 7))
 
 
 def swapped(shard, groups, axes):

time: 152 us -> 151 us (level)
  no operation moved by 1% of the time
where the time goes in v8:
time: 151 us
  blocking collectives  102 us (68%)
  starting transfers between devices  21.3 us (14%)
  Pallas kernels  13.8 us (9%)
  local copies, waits for them, and re-layouts  7.12 us (5%)
  waiting for transfers between devices  6.78 us (4%)
    all_to_all x3, blocking collectives, swapped(): lax.all_to_all(shard, axes, split_axis=0, concat_axis=0, axis_index_group...  102 us
    all_to_all x1, starting transfers between devices, swapped(): lax.all_to_all(shard, axes, split_axis=0, concat_axis=0, axis_index_group...  14.7 us
    pallas_call x1, Pallas kernels, dense(): pl.pallas_call(dense_kernel, grid=(steps,), in_specs=[SMEM, SMEM, *tiles]...  5.41 us
    unnamed x15, local copies, waits for them, and re-layouts  5.19 us
    pallas_call x1, Pallas kernels, forward(): pl.pallas_call(forward_kernel, in_specs=[SMEM] * 3 + [ANY, VMEM] + [ANY]...  4.7 us
    ppermute x2, starting transfers between devices, per_device(): other_tiles.append(lax.ppermute(piece, 'col', pairs))  4.32 us
    ppermute x2, waiting for transfers between devices, per_device(): other_tiles.append(lax.ppermute(piece, 'col', pairs))  3.55 us
    all_to_all x1, waiting for transfers between devices, swapped(): lax.all_to_all(shard, axes, split_axis=0, concat_axis=0, axis_index_group...  3.22 us
  transfers between devices with their start and end apart: 4, of which 3 were waited for; matrix products, arithmetic and copies ran while one was open for 1% of the time, Pallas kernels for 4%

profile of v8, /device:TPU:1, one launch (start us, length us, event | category | flops | bytes accessed | tf_op | source)
XLA Modules:
  0.0 150.9 jit_solution(11576571771822828226)
XLA Ops:
  0.0 0.0 copy-start.4
  0.0 0.8 copy-done.4
  0.8 0.0 copy-start.5
  0.8 0.0 copy-start.6
  0.8 0.0 copy-start.2
  0.8 0.1 shard_map.46
  0.9 0.0 copy-start.3
  0.9 1.1 copy-done.3
  2.0 14.7 %all-to-all-start = ((bf16[32,16,1024]{2,1,0:T(8,128)(2,1)}), bf16[32,16,1024]{2,1,0:T(8,128)(2,1)}, u32[]{:S(2)}, u32[]{:S(2)}) async-start(bf16[32,16,1024]{2,1,0:T(8,128)(2,1)} %bitcast.6), calls=%async_computation | async-start | bytes 2097152 | tf_op jit(solution)/shard_map/all_to_all | solution.py:20
  16.7 0.0 copy-done.5
  16.7 0.1 copy.5
  16.8 0.0 copy-done.6
  16.8 0.1 subtract_select_fusion.own_tab
  16.8 2.3 %collective-permute-start = (s32[8,3]{1,0:T(8,128)S(1)}, s32[8,3]{1,0:T(8,128)S(1)}, u32[]{:S(2)}, u32[]{:S(2)}) collective-permute-start(s32[8,3]{1,0:T(8,128)S(1)} %subtract_select_fusion.own_tab), channel_id=1, source_target_pairs={{0,1},{1,0},{2,3},{3,2},{4,5},{5,4},{6,7},{7,6},{8,9},{9,8},{10,11... | collective-permute-start | bytes 296 | tf_op jit(solution)/shard_map/ppermute | solution.py:262
  19.1 0.0 copy-done.2
  19.1 1.9 %fusion = (bf16[4,3,256,256]{3,2,1,0:T(8,128)(2,1)}, bf16[4,3,256,256]{3,2,1,0:T(8,128)(2,1)}) fusion(bf16[8,3,256,256]{3,2,1,0:T(8,128)(2,1)S(1)} %copy-done.2), kind=kLoop, calls=%fused_computation.2 | loop fusion | bytes 6291456 | tf_op jit(solution)/shard_map/split | solution.py:264
  21.1 0.0 collective-permute-done.other_tab
  21.1 2.0 %collective-permute-start.2 = (bf16[4,3,256,256]{3,2,1,0:T(8,128)(2,1)}, bf16[4,3,256,256]{3,2,1,0:T(8,128)(2,1)}, u32[]{:S(2)}, u32[]{:S(2)}) collective-permute-start(bf16[4,3,256,256]{3,2,1,0:T(8,128)(2,1)} %get-tuple-element.14), channel_id=1, source_target_pairs={{0,1},{1,0},{2,3},{3,2},{4,5},{5,4},{6,7},{7,6},{8,9},{9,8},{10,11... | collective-permute-start | bytes 4718600 | tf_op jit(solution)/shard_map/ppermute | solution.py:266
  23.1 2.3 %collective-permute-start.1 = (bf16[4,3,256,256]{3,2,1,0:T(8,128)(2,1)}, bf16[4,3,256,256]{3,2,1,0:T(8,128)(2,1)}, u32[]{:S(2)}, u32[]{:S(2)}) collective-permute-start(bf16[4,3,256,256]{3,2,1,0:T(8,128)(2,1)} %get-tuple-element.13), channel_id=1, source_target_pairs={{0,1},{1,0},{2,3},{3,2},{4,5},{5,4},{6,7},{7,6},{8,9},{9,8},{10,11... | collective-permute-start | bytes 4718600 | tf_op jit(solution)/shard_map/ppermute | solution.py:266
  25.4 1.3 collective-permute-done.2.refs_1_
  26.7 2.2 %collective-permute-done.1.refs_0_ = bf16[4,3,256,256]{3,2,1,0:T(8,128)(2,1)} collective-permute-done((bf16[4,3,256,256]{3,2,1,0:T(8,128)(2,1)}, bf16[4,3,256,256]{3,2,1,0:T(8,128)(2,1)}, u32[]{:S(2)}, u32[]{:S(2)}) %collective-permute-start.1) | collective-permute-done | bytes 1572896 | tf_op jit(solution)/shard_map/ppermute | solution.py:266
  28.9 5.4 %shard_map.47.factor_ref = bf16[8,2048,256]{2,1,0:T(8,128)(2,1)S(1)} custom-call(s32[8,3]{1,0:T(8,128)S(1)} %subtract_select_fusion.own_tab, s32[8,3]{1,0:T(8,128)S(1)} %collective-permute-done.other_tab, bf16[8,3,256,256]{3,2,1,0:T(8,128)(2,1)S(1)} %copy-done.2, bf16[4,3,256,256]{3,2,1,0:T(8,128)(2,1)} %collective-permute-done.1.refs_0_, ...), custom_call_target="tpu_custom_call" | custom-call | bytes 12582912 | tf_op jit(solution)/shard_map/pallas_call | solution.py:162
  34.4 0.0 copy-start
  34.4 3.2 %copy-done = bf16[8,2048,256]{2,1,0:T(8,128)(2,1)} copy-done((bf16[8,2048,256]{2,1,0:T(8,128)(2,1)}, bf16[8,2048,256]{2,1,0:T(8,128)(2,1)S(1)}, u32[]{:S(2)}) %copy-start) | copy-done | bytes 8388632
  37.6 3.2 %all-to-all-done = bf16[32,16,1024]{2,1,0:T(8,128)(2,1)} async-done(((bf16[32,16,1024]{2,1,0:T(8,128)(2,1)}), bf16[32,16,1024]{2,1,0:T(8,128)(2,1)}, u32[]{:S(2)}, u32[]{:S(2)}) %all-to-all-start) | async-done | bytes 1048608 | tf_op jit(solution)/shard_map/all_to_all | solution.py:20
  40.8 0.0 copy-start.1
  40.8 4.7 %shard_map.48 = s16[16,264,128]{2,1,0:T(8,128)(2,1)S(1)} custom-call(s32[1]{0:T(128)} %bitcast.core_ref, s32[8,3]{1,0:T(8,128)S(1)} %subtract_select_fusion.own_tab, s32[8,3]{1,0:T(8,128)S(1)} %collective-permute-done.other_tab, bf16[16,2,16,1024]{3,2,1,0:T(8,128)(2,1)} %bitcast.3.vec_source, bf16[8,3,256,256]{3,2,1,0:T(8,128)(2,1)S(1)} %copy-done.2, ...), custom_call_target="tpu_custom_call" | custom-call | flops 1610612736 | bytes 3145728 | tf_op jit(solution)/shard_map/pallas_call | solution.py:118
  45.5 36.4 %all_to_all.20.code_ref = s16[16,264,128]{2,1,0:T(8,128)(2,1)S(1)} all-to-all(s16[16,264,128]{2,1,0:T(8,128)(2,1)S(1)} %shard_map.48), channel_id=1, replica_groups={{6,28,14,18,26,22,8,10,24,16,2,0,30,12,4,20},{29,21,17,31,19,9,27,23,25..., dimensions={0} | all-to-all | bytes 2162688 | tf_op jit(solution)/shard_map/all_to_all | solution.py:20
  81.9 0.5 shard_map.49
  82.4 30.1 %all_to_all.21.row_ref = bf16[16,16,2048]{2,1,0:T(8,128)(2,1)S(1)} all-to-all(bf16[16,16,2048]{2,1,0:T(8,128)(2,1)S(1)} %shard_map.49), channel_id=1, replica_groups={{6,28,14,18,26,22,8,10,24,16,2,0,30,12,4,20},{29,21,17,31,19,9,27,23,25..., dimensions={0} | all-to-all | bytes 2097152 | tf_op jit(solution)/shard_map/all_to_all | solution.py:20
  112.5 0.0 copy-done.1
  112.5 2.3 %shard_map.50 = bf16[16,2,16,1024]{3,2,1,0:T(8,128)(2,1)S(1)} custom-call(s32[1]{0:T(128)} %bitcast.core_ref, bf16[16,16,2048]{2,1,0:T(8,128)(2,1)S(1)} %all_to_all.21.row_ref, bf16[8,2048,256]{2,1,0:T(8,128)(2,1)S(1)} %copy-done.1), custom_call_target="tpu_custom_call" | custom-call | flops 2147483648 | bytes 8388608 | tf_op jit(solution)/shard_map/pallas_call | solution.py:217
  114.9 35.2 %all_to_all.22 = bf16[32,16,1024]{2,1,0:T(8,128)(2,1)S(1)} all-to-all(bf16[32,16,1024]{2,1,0:T(8,128)(2,1)S(1)} %bitcast.8), channel_id=1, replica_groups={{448,449,320,321,256,257,480,481,288,289,128,129,416,417,352,353,384,38..., dimensions={0} | all-to-all | bytes 2097152 | tf_op jit(solution)/shard_map/all_to_all | solution.py:20
  150.1 0.8 shard_map.51
Async XLA Ops:
  0.0 0.8 copy-start.4
  0.8 15.8 %copy-start.5 = (s32[8,3]{0,1:T(4,128)S(1)}, s32[8,3]{0,1:T(4,128)}, u32[]{:S(2)}) copy-start(s32[8,3]{0,1:T(4,128)} %param.6) | copy-start | bytes 292
  0.8 15.9 %copy-start.6 = (s32[8,1]{0,1:T(1,128)S(1)}, s32[8,1]{0,1:T(1,128)}, u32[]{:S(2)}) copy-start(s32[8,1]{0,1:T(1,128)} %param.7) | copy-start | bytes 100
  0.8 18.3 %copy-start.2 = (bf16[8,3,256,256]{3,2,1,0:T(8,128)(2,1)S(1)}, bf16[8,3,256,256]{3,2,1,0:T(8,128)(2,1)}, u32[]{:S(2)}) copy-start(bf16[8,3,256,256]{3,2,1,0:T(8,128)(2,1)} %own_ref.3) | copy-start | bytes 9437188
  0.9 1.1 copy-start.3
  2.0 38.8 %all-to-all-start = ((bf16[32,16,1024]{2,1,0:T(8,128)(2,1)}), bf16[32,16,1024]{2,1,0:T(8,128)(2,1)}, u32[]{:S(2)}, u32[]{:S(2)}) async-start(bf16[32,16,1024]{2,1,0:T(8,128)(2,1)} %bitcast.6), calls=%async_computation | async-start | bytes 2097152 | tf_op jit(solution)/shard_map/all_to_all | solution.py:20
  16.8 4.2 %collective-permute-start = (s32[8,3]{1,0:T(8,128)S(1)}, s32[8,3]{1,0:T(8,128)S(1)}, u32[]{:S(2)}, u32[]{:S(2)}) collective-permute-start(s32[8,3]{1,0:T(8,128)S(1)} %subtract_select_fusion.own_tab), channel_id=1, source_target_pairs={{0,1},{1,0},{2,3},{3,2},{4,5},{5,4},{6,7},{7,6},{8,9},{9,8},{10,11... | collective-permute-start | bytes 296 | tf_op jit(solution)/shard_map/ppermute | solution.py:262
  21.1 5.6 %collective-permute-start.2 = (bf16[4,3,256,256]{3,2,1,0:T(8,128)(2,1)}, bf16[4,3,256,256]{3,2,1,0:T(8,128)(2,1)}, u32[]{:S(2)}, u32[]{:S(2)}) collective-permute-start(bf16[4,3,256,256]{3,2,1,0:T(8,128)(2,1)} %get-tuple-element.14), channel_id=1, source_target_pairs={{0,1},{1,0},{2,3},{3,2},{4,5},{5,4},{6,7},{7,6},{8,9},{9,8},{10,11... | collective-permute-start | bytes 4718600 | tf_op jit(solution)/shard_map/ppermute | solution.py:266
  23.1 5.8 %collective-permute-start.1 = (bf16[4,3,256,256]{3,2,1,0:T(8,128)(2,1)}, bf16[4,3,256,256]{3,2,1,0:T(8,128)(2,1)}, u32[]{:S(2)}, u32[]{:S(2)}) collective-permute-start(bf16[4,3,256,256]{3,2,1,0:T(8,128)(2,1)} %get-tuple-element.13), channel_id=1, source_target_pairs={{0,1},{1,0},{2,3},{3,2},{4,5},{5,4},{6,7},{7,6},{8,9},{9,8},{10,11... | collective-permute-start | bytes 4718600 | tf_op jit(solution)/shard_map/ppermute | solution.py:266
  34.4 3.2 %copy-start = (bf16[8,2048,256]{2,1,0:T(8,128)(2,1)}, bf16[8,2048,256]{2,1,0:T(8,128)(2,1)S(1)}, u32[]{:S(2)}) copy-start(bf16[8,2048,256]{2,1,0:T(8,128)(2,1)S(1)} %shard_map.47.factor_ref) | copy-start | bytes 25165828
  40.8 71.7 %copy-start.1 = (bf16[8,2048,256]{2,1,0:T(8,128)(2,1)S(1)}, bf16[8,2048,256]{2,1,0:T(8,128)(2,1)}, u32[]{:S(2)}) copy-start(bf16[8,2048,256]{2,1,0:T(8,128)(2,1)} %copy-done) | copy-start | bytes 25165828

commit v9 on v8

--- a/solution.py
+++ b/solution.py
@@ -12,7 +12,7 @@
 LANES = 128
 UNIT_BITS = 14
 PIECES = 2
-ROW_ORDER = (14, 10, 8, 15, 9, 4, 13, 11, 12, 1, 0, 3, 2, 6, 5, 7)
+ROW_ORDER = (4, 9, 7, 10, 1, 5, 15, 13, 12, 3, 2, 14, 11, 8, 0, 6)
 CHIP_ORDERS = ((3, 14, 7, 9, 13, 11, 4, 5, 12, 8, 1, 0, 15, 6, 2, 10), (14, 10, 8, 15, 9, 4, 13, 11, 12, 1, 0, 3, 2, 6, 5, 7))
 
 

time: 151 us -> 152 us (level)
  no operation moved by 1% of the time
where the time goes in v9:
time: 152 us
  blocking collectives  102 us (67%)
  starting transfers between devices  20.7 us (14%)
  Pallas kernels  13.8 us (9%)
  waiting for transfers between devices  7.84 us (5%)
  local copies, waits for them, and re-layouts  7.12 us (5%)
    all_to_all x3, blocking collectives, swapped(): lax.all_to_all(shard, axes, split_axis=0, concat_axis=0, axis_index_group...  102 us
    all_to_all x1, starting transfers between devices, swapped(): lax.all_to_all(shard, axes, split_axis=0, concat_axis=0, axis_index_group...  14.1 us
    pallas_call x1, Pallas kernels, dense(): pl.pallas_call(dense_kernel, grid=(steps,), in_specs=[SMEM, SMEM, *tiles]...  5.41 us
    unnamed x15, local copies, waits for them, and re-layouts  5.19 us
    pallas_call x1, Pallas kernels, forward(): pl.pallas_call(forward_kernel, in_specs=[SMEM] * 3 + [ANY, VMEM] + [ANY]...  4.7 us
    ppermute x2, starting transfers between devices, per_device(): other_tiles.append(lax.ppermute(piece, 'col', pairs))  4.32 us
    all_to_all x1, waiting for transfers between devices, swapped(): lax.all_to_all(shard, axes, split_axis=0, concat_axis=0, axis_index_group...  4.28 us
    ppermute x2, waiting for transfers between devices, per_device(): other_tiles.append(lax.ppermute(piece, 'col', pairs))  3.55 us
  transfers between devices with their start and end apart: 4, of which 3 were waited for; matrix products, arithmetic and copies ran while one was open for 1% of the time, Pallas kernels for 4%

profile of v9, /device:TPU:1, one launch (start us, length us, event | category | flops | bytes accessed | tf_op | source)
XLA Modules:
  0.0 151.9 jit_solution(2029078983643850613)
XLA Ops:
  0.0 0.0 copy-start.4
  0.0 0.8 copy-done.4
  0.8 0.0 copy-start.5
  0.8 0.0 copy-start.6
  0.8 0.0 copy-start.2
  0.8 0.1 shard_map.46
  0.9 0.0 copy-start.3
  0.9 1.1 copy-done.3
  2.0 14.1 %all-to-all-start = ((bf16[32,16,1024]{2,1,0:T(8,128)(2,1)}), bf16[32,16,1024]{2,1,0:T(8,128)(2,1)}, u32[]{:S(2)}, u32[]{:S(2)}) async-start(bf16[32,16,1024]{2,1,0:T(8,128)(2,1)} %bitcast.6), calls=%async_computation | async-start | bytes 2097152 | tf_op jit(solution)/shard_map/all_to_all | solution.py:20
  16.1 0.0 copy-done.5
  16.1 0.1 copy.5
  16.2 0.0 copy-done.6
  16.2 0.1 subtract_select_fusion.own_tab
  16.3 2.3 %collective-permute-start = (s32[8,3]{1,0:T(8,128)S(1)}, s32[8,3]{1,0:T(8,128)S(1)}, u32[]{:S(2)}, u32[]{:S(2)}) collective-permute-start(s32[8,3]{1,0:T(8,128)S(1)} %subtract_select_fusion.own_tab), channel_id=1, source_target_pairs={{0,1},{1,0},{2,3},{3,2},{4,5},{5,4},{6,7},{7,6},{8,9},{9,8},{10,11... | collective-permute-start | bytes 296 | tf_op jit(solution)/shard_map/ppermute | solution.py:262
  18.6 0.0 copy-done.2
  18.6 1.9 %fusion = (bf16[4,3,256,256]{3,2,1,0:T(8,128)(2,1)}, bf16[4,3,256,256]{3,2,1,0:T(8,128)(2,1)}) fusion(bf16[8,3,256,256]{3,2,1,0:T(8,128)(2,1)S(1)} %copy-done.2), kind=kLoop, calls=%fused_computation.2 | loop fusion | bytes 6291456 | tf_op jit(solution)/shard_map/split | solution.py:264
  20.5 0.0 collective-permute-done.other_tab
  20.5 2.0 %collective-permute-start.2 = (bf16[4,3,256,256]{3,2,1,0:T(8,128)(2,1)}, bf16[4,3,256,256]{3,2,1,0:T(8,128)(2,1)}, u32[]{:S(2)}, u32[]{:S(2)}) collective-permute-start(bf16[4,3,256,256]{3,2,1,0:T(8,128)(2,1)} %get-tuple-element.14), channel_id=1, source_target_pairs={{0,1},{1,0},{2,3},{3,2},{4,5},{5,4},{6,7},{7,6},{8,9},{9,8},{10,11... | collective-permute-start | bytes 4718600 | tf_op jit(solution)/shard_map/ppermute | solution.py:266
  22.6 2.3 %collective-permute-start.1 = (bf16[4,3,256,256]{3,2,1,0:T(8,128)(2,1)}, bf16[4,3,256,256]{3,2,1,0:T(8,128)(2,1)}, u32[]{:S(2)}, u32[]{:S(2)}) collective-permute-start(bf16[4,3,256,256]{3,2,1,0:T(8,128)(2,1)} %get-tuple-element.13), channel_id=1, source_target_pairs={{0,1},{1,0},{2,3},{3,2},{4,5},{5,4},{6,7},{7,6},{8,9},{9,8},{10,11... | collective-permute-start | bytes 4718600 | tf_op jit(solution)/shard_map/ppermute | solution.py:266
  24.8 1.3 collective-permute-done.2.refs_1_
  26.1 2.2 %collective-permute-done.1.refs_0_ = bf16[4,3,256,256]{3,2,1,0:T(8,128)(2,1)} collective-permute-done((bf16[4,3,256,256]{3,2,1,0:T(8,128)(2,1)}, bf16[4,3,256,256]{3,2,1,0:T(8,128)(2,1)}, u32[]{:S(2)}, u32[]{:S(2)}) %collective-permute-start.1) | collective-permute-done | bytes 1572896 | tf_op jit(solution)/shard_map/ppermute | solution.py:266
  28.4 5.4 %shard_map.47.factor_ref = bf16[8,2048,256]{2,1,0:T(8,128)(2,1)S(1)} custom-call(s32[8,3]{1,0:T(8,128)S(1)} %subtract_select_fusion.own_tab, s32[8,3]{1,0:T(8,128)S(1)} %collective-permute-done.other_tab, bf16[8,3,256,256]{3,2,1,0:T(8,128)(2,1)S(1)} %copy-done.2, bf16[4,3,256,256]{3,2,1,0:T(8,128)(2,1)} %collective-permute-done.1.refs_0_, ...), custom_call_target="tpu_custom_call" | custom-call | bytes 12582912 | tf_op jit(solution)/shard_map/pallas_call | solution.py:162
  33.8 0.0 copy-start
  33.8 3.2 %copy-done = bf16[8,2048,256]{2,1,0:T(8,128)(2,1)} copy-done((bf16[8,2048,256]{2,1,0:T(8,128)(2,1)}, bf16[8,2048,256]{2,1,0:T(8,128)(2,1)S(1)}, u32[]{:S(2)}) %copy-start) | copy-done | bytes 8388632
  37.0 4.3 %all-to-all-done = bf16[32,16,1024]{2,1,0:T(8,128)(2,1)} async-done(((bf16[32,16,1024]{2,1,0:T(8,128)(2,1)}), bf16[32,16,1024]{2,1,0:T(8,128)(2,1)}, u32[]{:S(2)}, u32[]{:S(2)}) %all-to-all-start) | async-done | bytes 1048608 | tf_op jit(solution)/shard_map/all_to_all | solution.py:20
  41.3 0.0 copy-start.1
  41.3 4.7 %shard_map.48 = s16[16,264,128]{2,1,0:T(8,128)(2,1)S(1)} custom-call(s32[1]{0:T(128)} %bitcast.core_ref, s32[8,3]{1,0:T(8,128)S(1)} %subtract_select_fusion.own_tab, s32[8,3]{1,0:T(8,128)S(1)} %collective-permute-done.other_tab, bf16[16,2,16,1024]{3,2,1,0:T(8,128)(2,1)} %bitcast.3.vec_source, bf16[8,3,256,256]{3,2,1,0:T(8,128)(2,1)S(1)} %copy-done.2, ...), custom_call_target="tpu_custom_call" | custom-call | flops 1610612736 | bytes 3145728 | tf_op jit(solution)/shard_map/pallas_call | solution.py:118
  46.0 36.7 %all_to_all.20.code_ref = s16[16,264,128]{2,1,0:T(8,128)(2,1)S(1)} all-to-all(s16[16,264,128]{2,1,0:T(8,128)(2,1)S(1)} %shard_map.48), channel_id=1, replica_groups={{6,28,14,18,26,22,8,10,24,16,2,0,30,12,4,20},{29,21,17,31,19,9,27,23,25..., dimensions={0} | all-to-all | bytes 2162688 | tf_op jit(solution)/shard_map/all_to_all | solution.py:20
  82.7 0.5 shard_map.49
  83.2 30.3 %all_to_all.21.row_ref = bf16[16,16,2048]{2,1,0:T(8,128)(2,1)S(1)} all-to-all(bf16[16,16,2048]{2,1,0:T(8,128)(2,1)S(1)} %shard_map.49), channel_id=1, replica_groups={{6,28,14,18,26,22,8,10,24,16,2,0,30,12,4,20},{29,21,17,31,19,9,27,23,25..., dimensions={0} | all-to-all | bytes 2097152 | tf_op jit(solution)/shard_map/all_to_all | solution.py:20
  113.5 0.0 copy-done.1
  113.5 2.3 %shard_map.50 = bf16[16,2,16,1024]{3,2,1,0:T(8,128)(2,1)S(1)} custom-call(s32[1]{0:T(128)} %bitcast.core_ref, bf16[16,16,2048]{2,1,0:T(8,128)(2,1)S(1)} %all_to_all.21.row_ref, bf16[8,2048,256]{2,1,0:T(8,128)(2,1)S(1)} %copy-done.1), custom_call_target="tpu_custom_call" | custom-call | flops 2147483648 | bytes 8388608 | tf_op jit(solution)/shard_map/pallas_call | solution.py:217
  115.9 35.2 %all_to_all.22 = bf16[32,16,1024]{2,1,0:T(8,128)(2,1)S(1)} all-to-all(bf16[32,16,1024]{2,1,0:T(8,128)(2,1)S(1)} %bitcast.8), channel_id=1, replica_groups={{128,129,288,289,224,225,320,321,32,33,160,161,480,481,416,417,384,385,..., dimensions={0} | all-to-all | bytes 2097152 | tf_op jit(solution)/shard_map/all_to_all | solution.py:20
  151.1 0.8 shard_map.51
Async XLA Ops:
  0.0 0.8 copy-start.4
  0.8 15.3 %copy-start.5 = (s32[8,3]{0,1:T(4,128)S(1)}, s32[8,3]{0,1:T(4,128)}, u32[]{:S(2)}) copy-start(s32[8,3]{0,1:T(4,128)} %param.6) | copy-start | bytes 292
  0.8 15.4 %copy-start.6 = (s32[8,1]{0,1:T(1,128)S(1)}, s32[8,1]{0,1:T(1,128)}, u32[]{:S(2)}) copy-start(s32[8,1]{0,1:T(1,128)} %param.7) | copy-start | bytes 100
  0.8 17.7 %copy-start.2 = (bf16[8,3,256,256]{3,2,1,0:T(8,128)(2,1)S(1)}, bf16[8,3,256,256]{3,2,1,0:T(8,128)(2,1)}, u32[]{:S(2)}) copy-start(bf16[8,3,256,256]{3,2,1,0:T(8,128)(2,1)} %own_ref.3) | copy-start | bytes 9437188
  0.9 1.1 copy-start.3
  2.0 39.3 %all-to-all-start = ((bf16[32,16,1024]{2,1,0:T(8,128)(2,1)}), bf16[32,16,1024]{2,1,0:T(8,128)(2,1)}, u32[]{:S(2)}, u32[]{:S(2)}) async-start(bf16[32,16,1024]{2,1,0:T(8,128)(2,1)} %bitcast.6), calls=%async_computation | async-start | bytes 2097152 | tf_op jit(solution)/shard_map/all_to_all | solution.py:20
  16.3 4.2 %collective-permute-start = (s32[8,3]{1,0:T(8,128)S(1)}, s32[8,3]{1,0:T(8,128)S(1)}, u32[]{:S(2)}, u32[]{:S(2)}) collective-permute-start(s32[8,3]{1,0:T(8,128)S(1)} %subtract_select_fusion.own_tab), channel_id=1, source_target_pairs={{0,1},{1,0},{2,3},{3,2},{4,5},{5,4},{6,7},{7,6},{8,9},{9,8},{10,11... | collective-permute-start | bytes 296 | tf_op jit(solution)/shard_map/ppermute | solution.py:262
  20.5 5.6 %collective-permute-start.2 = (bf16[4,3,256,256]{3,2,1,0:T(8,128)(2,1)}, bf16[4,3,256,256]{3,2,1,0:T(8,128)(2,1)}, u32[]{:S(2)}, u32[]{:S(2)}) collective-permute-start(bf16[4,3,256,256]{3,2,1,0:T(8,128)(2,1)} %get-tuple-element.14), channel_id=1, source_target_pairs={{0,1},{1,0},{2,3},{3,2},{4,5},{5,4},{6,7},{7,6},{8,9},{9,8},{10,11... | collective-permute-start | bytes 4718600 | tf_op jit(solution)/shard_map/ppermute | solution.py:266
  22.6 5.8 %collective-permute-start.1 = (bf16[4,3,256,256]{3,2,1,0:T(8,128)(2,1)}, bf16[4,3,256,256]{3,2,1,0:T(8,128)(2,1)}, u32[]{:S(2)}, u32[]{:S(2)}) collective-permute-start(bf16[4,3,256,256]{3,2,1,0:T(8,128)(2,1)} %get-tuple-element.13), channel_id=1, source_target_pairs={{0,1},{1,0},{2,3},{3,2},{4,5},{5,4},{6,7},{7,6},{8,9},{9,8},{10,11... | collective-permute-start | bytes 4718600 | tf_op jit(solution)/shard_map/ppermute | solution.py:266
  33.8 3.2 %copy-start = (bf16[8,2048,256]{2,1,0:T(8,128)(2,1)}, bf16[8,2048,256]{2,1,0:T(8,128)(2,1)S(1)}, u32[]{:S(2)}) copy-start(bf16[8,2048,256]{2,1,0:T(8,128)(2,1)S(1)} %shard_map.47.factor_ref) | copy-start | bytes 25165828
  41.3 72.2 %copy-start.1 = (bf16[8,2048,256]{2,1,0:T(8,128)(2,1)S(1)}, bf16[8,2048,256]{2,1,0:T(8,128)(2,1)}, u32[]{:S(2)}) copy-start(bf16[8,2048,256]{2,1,0:T(8,128)(2,1)} %copy-done) | copy-start | bytes 25165828
